TPU v7x, 32 devices: a whole 2x2x4 slice. The times are simulated.
32 devices in a mesh: dp: 16 (over z, x, core), tensor: 2 (over y).
Axes of the slice: x: 2, y: 2, z: 4, core: 2. Of those that a mesh axis runs over, the one named last changes fastest.
Arguments:
- patches: bfloat16 [25088, 1024], P('dp'), may hold values from -6 to 6
- cotangent: bfloat16 [25088, 1024], P('dp'), may hold values from -6 to 6
- clip_lengths: int32 [16, 8], P('dp'), may hold values from 0 to 1568, as said below
- attn_gain: float32 [1024], replicated, may hold values from 0.25 to 1.75
- attn_shift: float32 [1024], replicated, may hold values from -3 to 3
- qkv_weight: bfloat16 [1024, 3, 1024], P(None, None, 'tensor'), may hold values from -0.1875 to 0.1875
- qkv_bias: float32 [3, 1024], P(None, 'tensor'), may hold values from -3 to 3
- proj_weight: bfloat16 [1024, 1024], P('tensor'), may hold values from -2 to 2
- proj_bias: float32 [1024], replicated, may hold values from -3 to 3
- mlp_gain: float32 [1024], replicated, may hold values from 0.25 to 1.75
- mlp_shift: float32 [1024], replicated, may hold values from -3 to 3
- up_weight: bfloat16 [1024, 4096], P(None, 'tensor'), may hold values from -0.1875 to 0.1875
- up_bias: float32 [4096], P('tensor'), may hold values from -3 to 3
- down_weight: bfloat16 [4096, 1024], P('tensor'), may hold values from -0.09375 to 0.09375
- down_bias: float32 [1024], replicated, may hold values from -3 to 3
Outputs:
- block_out: bfloat16 [25088, 1024], P('dp')
- patch_grad: bfloat16 [25088, 1024], P('dp')
- attn_gain_grad: float32 [1024], replicated
- attn_shift_grad: float32 [1024], replicated
- qkv_weight_grad: float32 [1024, 3, 1024], P('dp', None, 'tensor')
- qkv_bias_grad: float32 [3, 1024], P(None, 'tensor')
- proj_weight_grad: float32 [1024, 1024], P('tensor', 'dp')
- proj_bias_grad: float32 [1024], replicated
- mlp_gain_grad: float32 [1024], replicated
- mlp_shift_grad: float32 [1024], replicated
- up_weight_grad: float32 [1024, 4096], P('dp', 'tensor')
- up_bias_grad: float32 [4096], P('tensor')
- down_weight_grad: float32 [4096, 1024], P('tensor', 'dp')
- down_bias_grad: float32 [1024], replicated
Inputs may be any that keep to these rules, and one draw needn't show every extreme that they name: `clip_lengths`: each row holds one index of dp: either one video of 1568 tokens followed by zeros, or 8 images of 196 tokens each; every draw has rows of both kinds.
All inputs are finite; a program needn't handle non-finite values.
Results may differ from a plain program's by a relative error of at most 0.015.
Values may be sent and summed in bfloat16 or wider, within the bound.
A program may use at most 448 MiB of HBM per device.

v0:
```python
import functools
import math

import jax
import jax.numpy as jnp
from jax import lax
from jax.experimental import pallas as pl
from jax.experimental.pallas import tpu as pltpu
from jax.sharding import PartitionSpec as P

HEAD_DIM = 64
HALF_DIM = HEAD_DIM // 2
GRID = 14
IMG = 196
EPS = 1e-06
SCALING = HEAD_DIM ** (-0.5)
LOG2E = math.log2(math.e)
KEY_CHUNKS = 2
MASK_ROWS = 16
ONES_ROWS = 16
FF_TILE = 512
FORBIDDEN = -1e30
VMEM_LIMIT = 62 * 1024 * 1024

MESH = pl.DeviceIdType.MESH

bf16 = jnp.bfloat16
f32 = jnp.float32


def dot(left, right, left_dim, right_dim):
    return lax.dot_general(
        left, right, (((left_dim,), (right_dim,)), ((), ())), preferred_element_type=f32
    )


def rotary_angles(offsets):
    pair_count = HALF_DIM
    side_pairs = pair_count * 11 // 32
    time_pairs = pair_count - 2 * side_pairs
    pair_index = jnp.arange(pair_count, dtype=jnp.int32)
    time_pair = pair_index < time_pairs
    height_pair = (pair_index >= time_pairs) & (pair_index < time_pairs + side_pairs)
    group_begin = jnp.where(
        time_pair, 0, jnp.where(height_pair, time_pairs, time_pairs + side_pairs)
    )
    group_size = jnp.where(time_pair, time_pairs, side_pairs)
    inverse = jnp.power(
        10000.0, -(pair_index - group_begin).astype(f32) / group_size.astype(f32)
    )
    frame_place = (offsets // IMG).astype(f32)
    row_place = (offsets % IMG // GRID).astype(f32)
    column_place = (offsets % GRID).astype(f32)
    position = jnp.where(
        time_pair[:, None],
        frame_place[None, :],
        jnp.where(height_pair[:, None], row_place[None, :], column_place[None, :]),
    )
    angles = position * inverse[:, None]
    return (jnp.cos(angles), jnp.sin(angles))


def params(collective_id=None):
    if collective_id is None:
        return pltpu.CompilerParams(vmem_limit_bytes=VMEM_LIMIT)
    return pltpu.CompilerParams(
        vmem_limit_bytes=VMEM_LIMIT, collective_id=collective_id, has_side_effects=True
    )


def greet(partners):
    barrier = pltpu.get_barrier_semaphore()
    for partner in partners:
        pl.semaphore_signal(barrier, inc=1, device_id=partner, device_id_type=MESH)
    pl.semaphore_wait(barrier, len(partners))


def partner_of(bit):
    index = lax.axis_index("dp")
    mine = (index // (1 << bit)) % 2
    return {"dp": index + (1 << bit) * (1 - 2 * mine)}, mine


def fold(keep, got, mine, next_keep, next_send):
    lead = (slice(None),) * (len(keep.shape) - 3)
    for pair in range(keep.shape[-3] // 2):
        for ref, odd in ((next_keep, mine), (next_send, 1 - mine)):
            at = lead + (2 * pair + odd,)
            value = keep[at]
            if got is not None:
                value = value.astype(f32) + got[at].astype(f32)
            ref[lead + (pair,)] = value.astype(bf16)


def remote(source, target, send_sem, recv_sem, partner):
    return pltpu.make_async_remote_copy(
        src_ref=source,
        dst_ref=target,
        send_sem=send_sem,
        recv_sem=recv_sem,
        device_id=partner,
        device_id_type=MESH,
    )


def whole_block(shape, **kwargs):
    return pl.BlockSpec(shape, lambda *_: (0,) * len(shape), **kwargs)


def once(shape):
    return whole_block(shape, pipeline_mode=pl.Buffered(1))


HBM = pl.BlockSpec(memory_space=pl.ANY)


def clamp(value, last):
    return jnp.minimum(jnp.maximum(value, 0), last)


def norm_parts(values):
    centre = values - jnp.mean(values, axis=1, keepdims=True)
    spread = jnp.mean(centre * centre, axis=1, keepdims=True)
    scale = lax.rsqrt(spread + EPS)
    return centre * scale, scale


def norm_back(grad, unit, scale, gain):
    c = grad * gain
    mean = jnp.mean(c, axis=1, keepdims=True)
    along = jnp.mean(c * unit, axis=1, keepdims=True)
    return scale * (c - mean - unit * along)


def column_sum(values):
    return jnp.sum(values, axis=0, keepdims=True)


def clip_masks(clip_len, tokens):
    token = jnp.arange(tokens, dtype=jnp.int32)[None, :] // IMG
    row = jnp.arange(MASK_ROWS, dtype=jnp.int32)[:, None]
    same = token == row
    images = clip_len < tokens
    forbid = images & jnp.logical_not(same) & (row < tokens // IMG)
    return jnp.where(forbid, FORBIDDEN, 0.0).astype(bf16), same.astype(bf16)


class Gather:
    STAGES = ((0,), (1, 2), (3, 4, 5, 6), (7, 8, 9, 10))
    COPIES = 11
    ROUTES = (
        (None, 0, 0, None),
        (0, 0, 0, 2),
        (1, 0, 0, 1),
        (0, 0, 0, 1),
        (0, 0, 1, 1),
        (1, 0, 0, 2),
        (1, 1, 0, 2),
        (None, 0, 0, 0),
        (None, 1, 0, 0),
        (None, 0, 1, 0),
        (None, 1, 1, 0),
    )

    def __init__(self, weight, other, send_sem, recv_sem):
        self.weight, self.other = weight, other
        self.send_sem, self.recv_sem = send_sem, recv_sem

    def place(self, x, z):
        core, mine_x, mine_z = (partner_of(bit)[1] for bit in range(3))
        x = mine_x + x * (1 - 2 * mine_x)
        return core + 2 * x + 4 * (mine_z + z * (1 - 2 * mine_z)), 8

    def copy(self, number):
        half, x, z, bit = self.ROUTES[number]
        index, parts = self.place(x, z)
        rows = self.other.shape[-2] // parts
        begin = index * rows
        if half is not None:
            rows //= 2
            begin = begin + half * rows
        at = (slice(None),) * (len(self.other.shape) - 2)
        at = at + (pl.ds(pl.multiple_of(begin, rows), rows),)
        source = self.weight if number == 0 else self.other
        return remote(
            source.at[at],
            self.other.at[at],
            self.send_sem.at[number],
            self.recv_sem.at[number],
            {"tensor": 1 - lax.axis_index("tensor")} if bit is None else partner_of(bit)[0],
        )

    def start(self, stage):
        for number in self.STAGES[stage]:
            self.copy(number).start()

    def wait(self, stage):
        for number in self.STAGES[stage]:
            self.copy(number).wait()

    def advance(self, stage):
        self.wait(stage - 1)
        self.start(stage)


class GatherZ(Gather):
    STAGES = ((0,), (1,), (2, 3))
    ROUTES = ((None, 0, 0, None), (None, 0, 0, 2), (None, 0, 0, 0), (None, 0, 1, 0))

    def place(self, x, z):
        core, mine_z = partner_of(0)[1], partner_of(2)[1]
        return core + 2 * (mine_z + z * (1 - 2 * mine_z)), 4


def neighbours():
    return [{"tensor": 1 - lax.axis_index("tensor")}] + [partner_of(bit)[0] for bit in range(3)]


def attend_kernel(
    x_ref,
    gain_ref,
    shift_ref,
    w_ref,
    b_ref,
    cos_ref,
    sin_ref,
    qm_ref,
    km_ref,
    proj_hbm,
    up_hbm,
    down_hbm,
    normed_ref,
    qkv_ref,
    att_ref,
    mine_ref,
    factor_ref,
    e_hbm,
    other_hbm,
    proj_other,
    up_other,
    down_other,
    k_scr,
    s_scr,
    e_scr,
    outgoing,
    e_sem,
    send_sem,
    recv_sem,
    gather_send,
    gather_recv,
):
    step, last = pl.program_id(0), pl.num_programs(0) - 1
    tokens, width = x_ref.shape
    half = tokens // 2
    chunk = tokens // KEY_CHUNKS
    heads = e_hbm.shape[0]
    side = lax.axis_index("tensor")
    peer = {"tensor": 1 - side}
    proj = Gather(proj_hbm, proj_other, gather_send.at[0], gather_recv.at[0])
    up = Gather(up_hbm, up_other, gather_send.at[1], gather_recv.at[1])
    down = Gather(down_hbm, down_other, gather_send.at[2], gather_recv.at[2])

    @pl.when(step == 0)
    def _():
        greet(neighbours())
        proj.start(0)
        up.start(0)
        unit, _ = norm_parts(x_ref[...].astype(f32))
        normed_ref[:width] = (unit * gain_ref[...] + shift_ref[...]).astype(bf16).T
        normed_ref[width:] = jnp.ones((ONES_ROWS, tokens), bf16)

    for at, weight, stage in (
        (2, proj, 1),
        (3, down, 0),
        (4, proj, 2),
        (4, up, 1),
        (6, proj, 3),
        (6, up, 2),
        (9, up, 3),
    ):

        @pl.when(step == at)
        def _():
            if stage:
                weight.advance(stage)
            else:
                weight.start(stage)

    @pl.when(step < 3)
    def _():
        rows = w_ref.shape[2]
        bias = jnp.broadcast_to(b_ref[pl.ds(step, 1), :], (8, rows)).T[:, :1]
        mixed = dot(w_ref[0], normed_ref[:width], 0, 0) + bias

        @pl.when(step < 2)
        def _():
            cosine, sine = cos_ref[...], sin_ref[...]
            for begin in range(0, rows, HEAD_DIM):
                middle, end = begin + HALF_DIM, begin + HEAD_DIM
                low, high = mixed[begin:middle], mixed[middle:end]
                qkv_ref[step, begin:middle, :] = (low * cosine - high * sine).astype(bf16)
                qkv_ref[step, middle:end, :] = (high * cosine + low * sine).astype(bf16)

        @pl.when(step == 2)
        def _():
            qkv_ref[step] = mixed.astype(bf16)

    head = step - 3
    slot = head % 2

    def store(index, part):
        at = pl.ds(part * chunk, chunk)
        return pltpu.make_async_copy(
            e_scr.at[index % 2, at], e_hbm.at[index, at], e_sem.at[index % 2, part]
        )

    def exchange(index):
        at = pl.ds(pl.multiple_of(index * HEAD_DIM, HEAD_DIM), HEAD_DIM)
        return remote(
            outgoing.at[index],
            other_hbm.at[at],
            send_sem.at[index],
            recv_sem.at[index],
            peer,
        )

    @pl.when(head >= 2)
    def _():
        for part in range(KEY_CHUNKS):
            store(head - 2, part).wait()

    @pl.when(head >= 0)
    def _():
        at = pl.ds(pl.multiple_of(clamp(head, heads - 1) * HEAD_DIM, HEAD_DIM), HEAD_DIM)
        queries = jnp.concatenate([qkv_ref[0, at], qm_ref[...]], axis=0)
        k_scr[...] = jnp.concatenate([qkv_ref[1, at], km_ref[...]], axis=0).T
        values = jnp.concatenate([qkv_ref[2, at], jnp.ones((16, tokens), bf16)], axis=0)
        top, out, tops = None, None, []
        s_scr[0] = dot(k_scr[:chunk], queries, 1, 0)
        for part in range(KEY_CHUNKS):
            begin, end = part * chunk, (part + 1) * chunk
            if part + 1 < KEY_CHUNKS:
                s_scr[(part + 1) % 2] = dot(k_scr[end : end + chunk], queries, 1, 0)
            scores = s_scr[part % 2]
            here = jnp.max(scores, axis=0, keepdims=True)
            new_top = here if top is None else jnp.maximum(top, here)
            weights = jnp.exp2((scores - new_top) * (SCALING * LOG2E)).astype(bf16)
            e_scr[slot, begin:end] = weights
            store(head, part).start()
            term = dot(values[:, begin:end], weights, 1, 0)
            if out is None:
                out = term
            else:
                out = out * jnp.exp2((top - new_top) * (SCALING * LOG2E)) + term
            top = new_top
            tops.append(top)
        scale = 1.0 / out[HEAD_DIM : HEAD_DIM + 1]
        for part in range(KEY_CHUNKS):
            factor_ref[0, part : part + 1] = scale * jnp.exp2(
                (tops[part] - top) * (SCALING * LOG2E)
            )
        attended = out[:HEAD_DIM] * scale
        att_ref[...] = attended.astype(bf16)
        left, right = attended[:, :half], attended[:, half:]
        mine_ref[...] = jnp.where(side == 0, left, right).astype(bf16)
        outgoing[clamp(head, heads - 1)] = jnp.where(side == 0, right, left).astype(bf16)
        exchange(head).start()

    @pl.when(step == last)
    def _():
        for back in (2, 1):
            for part in range(KEY_CHUNKS):
                store(heads - back, part).wait()
        for index in range(heads):
            exchange(index).wait()
        for weight, stage in ((proj, 3), (up, 3), (down, 0)):
            weight.wait(stage)


def attend_forward(
    patches, gain, shift, weight, bias, cosine, sine, query_mask, key_mask, proj, up, down
):
    tokens, width = patches.shape
    columns = weight.shape[2]
    heads = columns // HEAD_DIM
    half = tokens // 2
    head = lambda i: clamp(i - 3, heads - 1)
    vmem = pltpu.VMEM
    dma = lambda *shape: pltpu.SemaphoreType.DMA(shape)
    return pl.pallas_call(
        attend_kernel,
        grid=(3 + heads,),
        out_shape=(
            jax.ShapeDtypeStruct((width + ONES_ROWS, tokens), bf16),
            jax.ShapeDtypeStruct((3, columns, tokens), bf16),
            jax.ShapeDtypeStruct((columns, tokens), bf16),
            jax.ShapeDtypeStruct((columns, half), bf16),
            jax.ShapeDtypeStruct((heads, KEY_CHUNKS, tokens), f32),
            jax.ShapeDtypeStruct((heads, tokens, tokens), bf16),
            jax.ShapeDtypeStruct((columns, half), bf16),
            jax.ShapeDtypeStruct(proj.shape, bf16),
            jax.ShapeDtypeStruct(up.shape, bf16),
            jax.ShapeDtypeStruct(down.shape, bf16),
        ),
        in_specs=[
            once((tokens, width)),
            once((1, width)),
            once((1, width)),
            pl.BlockSpec((1, width, columns), lambda i: (clamp(i, 2), 0, 0)),
            once((3, columns)),
            once(cosine.shape),
            once(sine.shape),
            once(query_mask.shape),
            once(key_mask.shape),
            HBM,
            HBM,
            HBM,
        ],
        out_specs=(
            once((width + ONES_ROWS, tokens)),
            once((3, columns, tokens)),
            pl.BlockSpec((HEAD_DIM, tokens), lambda i: (head(i), 0)),
            pl.BlockSpec((HEAD_DIM, half), lambda i: (head(i), 0)),
            pl.BlockSpec((1, KEY_CHUNKS, tokens), lambda i: (head(i), 0, 0)),
            HBM,
            HBM,
            HBM,
            HBM,
            HBM,
        ),
        scratch_shapes=[
            vmem((tokens, HEAD_DIM + MASK_ROWS), bf16),
            vmem((2, tokens // KEY_CHUNKS, tokens), f32),
            vmem((2, tokens, tokens), bf16),
            vmem((heads, HEAD_DIM, half), bf16),
            dma(2, KEY_CHUNKS),
            dma(heads),
            dma(heads),
            dma(3, Gather.COPIES),
            dma(3, Gather.COPIES),
        ],
        compiler_params=params(3),
        cost_estimate=pl.CostEstimate(
            flops=6 * tokens * width * columns + 16 * heads * tokens * tokens * HEAD_DIM,
            bytes_accessed=60_000_000,
            transcendentals=heads * tokens * tokens,
        ),
        name="attend_forward",
    )(
        patches,
        gain[None, :],
        shift[None, :],
        weight,
        bias,
        cosine,
        sine,
        query_mask,
        key_mask,
        proj,
        up,
        down,
    )


def attend_back_kernel(
    e_ref,
    q_ref,
    k_ref,
    v_ref,
    out_ref,
    total_ref,
    att_grad_ref,
    cos_ref,
    sin_ref,
    normed_ref,
    down_keep_ref,
    down_got_ref,
    up_keep_ref,
    up_got_ref,
    att_send_hbm,
    _,
    mine_ref,
    keep_ref,
    sum_ref,
    down_sum_ref,
    up_sum_ref,
    other_ref,
    got_ref,
    att_got_hbm,
    att_scr,
    up_scr,
    up_low,
    value_scr,
    v_scr,
    score_grad,
    turned,
    pair_scr,
    outgoing,
    grad,
    outgoing_core,
    down_scr,
    down_last,
    up_first,
    up_last,
    send_sem,
    recv_sem,
    core_send,
    core_recv,
    down_sem,
    down_last_sem,
    up_sem,
    up_last_sem,
    att_sem,
    att_load_sem,
):
    head, heads = pl.program_id(0), pl.num_programs(0)
    tokens = q_ref.shape[2]
    half = tokens // 2
    side = lax.axis_index("tensor")
    peer = {"tensor": 1 - side}
    core_partner, core = partner_of(0)
    slot = head % 2
    def exchange(index):
        return remote(
            outgoing.at[index % 4],
            other_ref.at[index],
            send_sem.at[index % 4],
            recv_sem.at[index],
            peer,
        )

    def to_core(pair):
        at = pl.ds(pl.multiple_of(pair * 2 * HEAD_DIM, 2 * HEAD_DIM), 2 * HEAD_DIM)
        return remote(
            outgoing_core.at[pair % 2],
            got_ref.at[:, :, :, at],
            core_send.at[pair % 2],
            core_recv.at[pair],
            core_partner,
        )

    def hop(buffers, sems, pair, bit):
        at = pl.ds(2 * pair, 2)
        return remote(
            buffers.at[1, at],
            buffers.at[2, at],
            sems.at[0, pair],
            sems.at[1, pair],
            partner_of(bit)[0],
        )

    def start(keep, got, buffers, sems, pair, bit):
        at = pl.ds(2 * pair, 2)
        fold(keep, got, partner_of(bit)[1], buffers.at[0, at], buffers.at[1, at])
        hop(buffers, sems, pair, bit).start()

    def relay(source, source_sems, source_bit, buffers, sems, pair, bit):
        hop(source, source_sems, pair, source_bit).wait_recv()
        at = pl.ds(2 * pair, 2)
        start(source.at[0, at], source.at[2, at], buffers, sems, pair, bit)

    down_pairs, up_pairs = down_scr.shape[1] // 2, up_first.shape[1] // 2
    behind = heads - up_pairs

    late_heads = pl.ds(att_got_hbm.shape[0] // 2, att_got_hbm.shape[0] // 2)
    att_far = remote(
        att_send_hbm.at[late_heads], att_got_hbm.at[late_heads], att_sem.at[0], att_sem.at[1], peer
    )

    def att_load(index):
        at = pl.ds(pl.multiple_of(index * HEAD_DIM, HEAD_DIM), HEAD_DIM)
        return pltpu.make_async_copy(
            att_got_hbm.at[at], att_scr.at[index % 2], att_load_sem.at[index % 2]
        )

    @pl.when(head == 0)
    def _():
        att_load(0).start()
        greet(neighbours() + [partner_of(3)[0]])
        att_far.start()

    @pl.when(head >= 4)
    def _():
        exchange(head - 4).wait_send()

    @pl.when(head < up_pairs)
    def _():
        start(up_keep_ref, up_got_ref, up_first, up_sem, head, 1)

    @pl.when(head < down_pairs)
    def _():
        start(down_keep_ref, down_got_ref, down_scr, down_sem, head, 2)

    @pl.when(head >= heads - down_pairs)
    def _():
        relay(
            down_scr, down_sem, 2, down_last, down_last_sem, head - (heads - down_pairs), 3
        )

    @pl.when(head >= behind)
    def _():
        relay(up_first, up_sem, 1, up_last, up_last_sem, head - behind, 2)

    @pl.when(head + 1 == heads // 2)
    def _():
        att_far.wait_recv()

    @pl.when(head + 1 < heads)
    def _():
        att_load(head + 1).start()

    att_load(head).wait()
    chunks = total_ref.shape[1]
    chunk = tokens // chunks
    att_mine, att_other = att_grad_ref[...].astype(f32), att_scr[slot].astype(f32)
    up_scr[:, :half] = jnp.where(side == 0, att_mine, att_other)
    up_scr[:, half:] = jnp.where(side == 0, att_other, att_mine)
    attended = out_ref[...].astype(f32)
    centre = []
    for part in range(chunks):
        up_low[part] = (up_scr[...] * total_ref[0, part : part + 1]).astype(bf16)
        centre.append(column_sum(up_low[part].astype(f32) * attended))
    v_scr[...] = v_ref[0].T
    cosine, sine = cos_ref[...], sin_ref[...]

    def store(part, low, high):
        for row, value in ((0, low), (HALF_DIM, high)):
            left, right = value[:, :half], value[:, half:]
            mine_ref[part, row : row + HALF_DIM] = jnp.where(side == 0, left, right).astype(bf16)
            outgoing[head % 4, part, row : row + HALF_DIM] = jnp.where(
                side == 0, right, left
            ).astype(bf16)
            begin = pl.multiple_of(part * 2 * HEAD_DIM + slot * HEAD_DIM + row, HALF_DIM)
            pair_scr[pl.ds(begin, HALF_DIM)] = value.astype(bf16)

    def unrotated(part, grad):
        low, high = grad[:HALF_DIM] * SCALING, grad[HALF_DIM:] * SCALING
        store(part, low * cosine + high * sine, high * cosine - low * sine)

    for part in range(chunks):
        at = slice(part * chunk, (part + 1) * chunk)
        value_scr[:, at] = dot(up_low[part], e_ref[0, at], 1, 1)
        prob_grad = dot(v_scr[at], up_low[part], 1, 0)
        score_grad[at] = (e_ref[0, at].astype(f32) * (prob_grad - centre[part])).astype(bf16)
    store(2, value_scr[:HALF_DIM], value_scr[HALF_DIM:])
    unrotated(0, dot(k_ref[0], score_grad[...], 1, 0))
    turned[...] = score_grad[...].T
    unrotated(1, dot(q_ref[0], turned[...], 1, 0))
    exchange(head).start()

    @pl.when(slot == 1)
    def _():
        pair = head // 2
        width = grad.shape[0] - ONES_ROWS
        grad[...] = dot(normed_ref[...], pair_scr[...], 1, 1)

        @pl.when(pair >= 2)
        def _():
            to_core(pair - 2).wait_send()

        for part in range(3):
            lanes = pl.ds(part * 2 * HEAD_DIM, 2 * HEAD_DIM)
            split_rows(
                grad.at[:, lanes], keep_ref.at[part], outgoing_core.at[pair % 2, part], core
            )
            sum_ref[part : part + 1] = grad[width : width + 1, lanes]
        to_core(pair).start()

    @pl.when(head == heads - 1)
    def _():
        for back in range(4):
            exchange(heads - 1 - back).wait_send()
        for back in range(2):
            to_core(heads // 2 - 1 - back).wait_send()
        for index in range(other_ref.shape[0] // 2):
            to_core(index).wait_recv()
        for pair in range(down_pairs):
            hop(down_scr, down_sem, pair, 2).wait_send()
            hop(down_last, down_last_sem, pair, 3).wait()
        down_sum_ref[...] = down_last[0].astype(f32) + down_last[2].astype(f32)
        for pair in range(up_pairs):
            hop(up_first, up_sem, pair, 1).wait_send()
            hop(up_last, up_last_sem, pair, 2).wait()
        up_sum_ref[...] = (up_last[0].astype(f32) + up_last[2].astype(f32)).astype(bf16)
        att_far.wait_send()
        for index in range(other_ref.shape[0]):
            exchange(index).wait_recv()


def attend_backward(
    count,
    weights,
    qkv,
    attended,
    totals,
    att_grad,
    att_send,
    att_got,
    cosine,
    sine,
    normed,
    down_keep,
    down_got,
    up_keep,
    up_got,
):
    tokens = qkv.shape[2]
    half = tokens // 2
    heads = weights.shape[0]
    columns = heads * HEAD_DIM
    width = normed.shape[0] - ONES_ROWS
    rows = width // count
    split = (3, count // 2, rows)
    blocks = lambda bits: (count >> bits, rows, FF_TILE)
    pair = lambda lead, first, last: pl.BlockSpec(
        (2,) + lead, lambda i: (first + clamp(i, last), 0, 0, 0)
    )
    block = lambda part: pl.BlockSpec((1, HEAD_DIM, tokens), lambda i: (part, i, 0))
    half_block = pl.BlockSpec((HEAD_DIM, half), lambda i: (i, 0))
    pair_block = pl.BlockSpec(split + (2 * HEAD_DIM,), lambda i: (0, 0, 0, i // 2))
    vmem = pltpu.VMEM
    dma = lambda *shape: pltpu.SemaphoreType.DMA(shape)
    return pl.pallas_call(
        attend_back_kernel,
        grid=(heads,),
        out_shape=(
            jax.ShapeDtypeStruct((3, columns, half), bf16),
            jax.ShapeDtypeStruct(split + (columns,), bf16),
            jax.ShapeDtypeStruct((3, columns), f32),
            jax.ShapeDtypeStruct((heads,) + blocks(4), f32),
            jax.ShapeDtypeStruct((heads + 2,) + blocks(3), bf16),
            jax.ShapeDtypeStruct((heads, 3, HEAD_DIM, half), bf16),
            jax.ShapeDtypeStruct(split + (columns,), bf16),
            jax.ShapeDtypeStruct(att_got.shape, bf16),
        ),
        input_output_aliases={15: 7},
        in_specs=[
            pl.BlockSpec((1, tokens, tokens), lambda i: (i, 0, 0)),
            block(0),
            block(1),
            block(2),
            pl.BlockSpec((HEAD_DIM, tokens), lambda i: (i, 0)),
            pl.BlockSpec((1, totals.shape[1], tokens), lambda i: (i, 0, 0)),
            half_block,
            once(cosine.shape),
            once(sine.shape),
            once(normed.shape),
            pair(blocks(2), 0, heads // 2 - 1),
            pair(blocks(2), 0, heads // 2 - 1),
            pair(blocks(1), 0, heads // 2),
            pair(blocks(1), heads // 2, heads // 2),
            HBM,
            HBM,
        ],
        out_specs=(
            pl.BlockSpec((3, HEAD_DIM, half), lambda i: (0, i, 0)),
            pair_block,
            pl.BlockSpec((3, 2 * HEAD_DIM), lambda i: (0, i // 2)),
            once((heads,) + blocks(4)),
            once((heads + 2,) + blocks(3)),
            HBM,
            HBM,
            HBM,
        ),
        scratch_shapes=[
            vmem((2, HEAD_DIM, half), bf16),
            vmem((HEAD_DIM, tokens), f32),
            vmem((totals.shape[1], HEAD_DIM, tokens), bf16),
            vmem((HEAD_DIM, tokens), f32),
            vmem((tokens, HEAD_DIM), bf16),
            vmem((tokens, tokens), bf16),
            vmem((tokens, tokens), bf16),
            vmem((6 * HEAD_DIM, tokens), bf16),
            vmem((4, 3, HEAD_DIM, half), bf16),
            vmem((width + ONES_ROWS, 6 * HEAD_DIM), f32),
            vmem((2,) + split + (2 * HEAD_DIM,), bf16),
            vmem((3, heads) + blocks(3), bf16),
            vmem((3, heads) + blocks(4), bf16),
            vmem((3, heads + 2) + blocks(2), bf16),
            vmem((3, heads + 2) + blocks(3), bf16),
            dma(4),
            dma(heads),
            dma(2),
            dma(heads // 2),
            dma(2, heads // 2),
            dma(2, heads // 2),
            dma(2, heads // 2 + 1),
            dma(2, heads // 2 + 1),
            dma(2),
            dma(2),
        ],
        compiler_params=params(0),
        cost_estimate=pl.CostEstimate(
            flops=32 * heads * tokens * tokens * HEAD_DIM,
            bytes_accessed=2 * heads * tokens * tokens,
            transcendentals=0,
        ),
        name="attend_backward",
    )(
        weights,
        qkv,
        qkv,
        qkv,
        attended,
        totals,
        att_grad,
        cosine,
        sine,
        normed,
        down_keep,
        down_got,
        up_keep,
        up_got,
        att_send,
        att_got,
    )


def normal_parts(value):
    a = jnp.abs(value)
    t = 1.0 / (1.0 + (0.3275911 / math.sqrt(2.0)) * a)
    bell = jnp.exp2(value * value * (-0.5 * LOG2E))
    c = [0.5 * x for x in (0.254829592, -0.284496736, 1.421413741, -1.453152027, 1.061405429)]
    tail = ((((c[4] * t + c[3]) * t + c[2]) * t + c[1]) * t + c[0]) * t * bell
    return jnp.where(value >= 0, 1.0 - tail, tail), bell * (1.0 / math.sqrt(2.0 * math.pi))


def split_rows(grad, keep_ref, send_ref, core):
    count, rows = keep_ref.shape[:2]
    for pair in range(count):
        for ref, odd in ((keep_ref, core), (send_ref, 1 - core)):
            begin = pl.multiple_of((2 * pair + odd) * rows, rows)
            ref[pair] = grad[pl.ds(begin, rows), :].astype(bf16)


def accumulate(step, total, term):
    @pl.when(step == 0)
    def _():
        total[...] = term

    @pl.when(step > 0)
    def _():
        total[...] += term


def feed_kernel(
    att_ref,
    att_other_ref,
    proj_ref,
    proj_other_ref,
    proj_bias_ref,
    gain_ref,
    shift_ref,
    down_bias_ref,
    up_bias_ref,
    patch_hbm,
    cot_hbm,
    up_hbm,
    up_other_hbm,
    down_hbm,
    _,
    qkv_hbm,
    grad_ref,
    att_grad_ref,
    att_scr,
    vector_ref,
    up_bias_grad_ref,
    keep_x_ref,
    keep_ref,
    out_hbm,
    att_got_hbm,
    got_hbm,
    got_x_hbm,
    down_other_hbm,
    qkv_other_hbm,
    n_scr,
    cot_scr,
    out_scr,
    total,
    act_scr,
    slope_scr,
    up_scr,
    down_scr,
    low_scr,
    grad_scr,
    keep_ring,
    outgoing,
    arrived,
    outgoing_x,
    load_sem,
    up_sem,
    down_sem,
    store_sem,
    row_sem,
    att_sem,
    send_sem,
    recv_sem,
    arrive_sem,
    send_x_sem,
    recv_x_sem,
    gather_send,
    gather_recv,
):
    step, last = pl.program_id(0), pl.num_programs(0) - 1
    tiles = act_scr.shape[0]
    half_tiles = tiles // 2
    half = n_scr.shape[0]
    side = lax.axis_index("tensor")
    peer = {"tensor": 1 - side}
    core_partner, core = partner_of(0)
    x_partner, x_side = partner_of(1)
    mine = pl.ds(pl.multiple_of(side * half, 16), half)
    gather_down = Gather(down_hbm, down_other_hbm, gather_send.at[0], gather_recv.at[0])
    gather_qkv = GatherZ(qkv_hbm, qkv_other_hbm, gather_send.at[1], gather_recv.at[1])
    patch_load = pltpu.make_async_copy(patch_hbm.at[mine], out_scr, load_sem.at[0])
    cot_load = pltpu.make_async_copy(cot_hbm.at[mine], cot_scr, load_sem.at[1])
    out_near = pltpu.make_async_copy(out_scr, out_hbm.at[mine], store_sem)
    out_far = remote(out_scr, out_hbm.at[mine], row_sem.at[0], row_sem.at[1], peer)
    early_heads = pl.ds(0, att_scr.shape[0] // 2)
    att_far = remote(
        att_scr.at[early_heads], att_got_hbm.at[early_heads], att_sem.at[0], att_sem.at[1], peer
    )

    def load_up(tile, act):
        for begin, source in ((0, up_hbm), (half_tiles, up_other_hbm)):

            @pl.when((tile >= begin) & (tile < begin + half_tiles))
            def _():
                at = pl.ds(pl.multiple_of((tile - begin) * FF_TILE, FF_TILE), FF_TILE)
                copy = pltpu.make_async_copy(
                    source.at[:, at], up_scr.at[tile % 2], up_sem.at[tile % 2]
                )
                getattr(copy, act)()

    def load_down(tile, act):
        for begin, source in ((0, down_hbm), (half_tiles, down_other_hbm)):

            @pl.when((tile >= begin) & (tile < begin + half_tiles))
            def _():
                at = pl.ds(pl.multiple_of((tile - begin) * FF_TILE, FF_TILE), FF_TILE)
                copy = pltpu.make_async_copy(
                    source.at[at], down_scr.at[tile % 2], down_sem.at[tile % 2]
                )
                getattr(copy, act)()

    def to_core(index):
        return remote(
            outgoing.at[index % 2],
            got_hbm.at[index],
            send_sem.at[index % 2],
            recv_sem.at[index],
            core_partner,
        )

    def to_x(index):
        return remote(
            outgoing_x.at[index],
            got_x_hbm.at[index],
            send_x_sem.at[index],
            recv_x_sem.at[index],
            x_partner,
        )

    def arrive(index):
        return pltpu.make_async_copy(
            got_hbm.at[index], arrived.at[index % 2], arrive_sem.at[index % 2]
        )

    @pl.when(step == 0)
    def _():
        patch_load.start()
        cot_load.start()
        load_up(0, "start")
        greet(neighbours())
        gather_down.start(1)
        gather_qkv.start(0)
        branch = dot(att_ref[...], proj_ref[...], 0, 0).astype(bf16).astype(f32)
        other = dot(att_other_ref[...], proj_other_ref[...], 0, 0).astype(bf16).astype(f32)
        patch_load.wait()
        residual = out_scr[...].astype(f32) + (branch + other + proj_bias_ref[...])
        grad_ref[...] = residual
        unit, _ = norm_parts(residual)
        n_scr[...] = (unit * gain_ref[...] + shift_ref[...]).astype(bf16)
        cot_load.wait()
        vector_ref[3:4] = column_sum(cot_scr[...].astype(f32))

    slot = step % 2

    for at, weight, stage in (
        (half_tiles - 1, gather_down, 2),
        (tiles, gather_down, 3),
        (tiles + 4, gather_qkv, 1),
        (2 * tiles + 4, gather_qkv, 2),
    ):

        @pl.when(step == at)
        def _():
            weight.advance(stage)

    @pl.when(step == tiles + half_tiles - 1)
    def _():
        gather_down.wait(3)

    first, second, third = step, step - tiles, step - 2 * tiles

    @pl.when(first + 1 < tiles)
    def _():
        load_up(first + 1, "start")

    @pl.when(first < tiles)
    def _():
        load_up(first, "wait")

    @pl.when((second + 1 >= 0) & (second + 1 < tiles))
    def _():
        load_down(second + 1, "start")

    @pl.when((second >= 0) & (second < tiles))
    def _():
        load_down(second, "wait")

    @pl.when((third + 1 >= 0) & (third + 1 < tiles))
    def _():
        load_up(third + 1, "start")
        load_down(third + 1, "start")

    @pl.when((third >= 0) & (third < tiles))
    def _():
        load_up(third, "wait")
        load_down(third, "wait")

    item = jnp.where(step < tiles, step, step - 2 * tiles)
    sends = (step < tiles) | (step >= 3 * tiles)

    @pl.when(sends & (item >= 2))
    def _():
        to_core(item - 2).wait_send()

    def send_gradient(value, keep):
        grad_scr[...] = value
        split_rows(grad_scr, keep, outgoing.at[slot], core)
        to_core(item).start()

    @pl.when(first < tiles)
    def _():
        upward = dot(n_scr[...], up_scr[slot], 1, 0) + up_bias_ref[clamp(first, tiles - 1)]
        share, density = normal_parts(upward)
        activated = (upward * share).astype(bf16)
        act_scr[clamp(first, tiles - 1)] = activated
        slope_scr[clamp(first, tiles - 1)] = (share + upward * density).astype(bf16)
        send_gradient(dot(cot_scr[...], activated, 0, 0), keep_ring.at[clamp(first, tiles - 1)])

    @pl.when((second >= 0) & (second < tiles))
    def _():
        accumulate(second, total, dot(act_scr[clamp(second, tiles - 1)], down_scr[slot], 1, 0))

    @pl.when(second == tiles - 1)
    def _():
        out_scr[...] = (grad_ref[...] + (total[...] + down_bias_ref[...])).astype(bf16)
        out_near.start()
        out_far.start()

    @pl.when((third >= 0) & (third < tiles))
    def _():
        tile = clamp(third, tiles - 1)
        act_grad = dot(cot_scr[...], down_scr[slot], 1, 1)
        upward_grad = (act_grad * slope_scr[tile].astype(f32)).astype(bf16)
        slope_scr[tile] = upward_grad
        up_bias_grad_ref[0] = column_sum(upward_grad.astype(f32))
        accumulate(third, total, dot(upward_grad, up_scr[slot], 1, 1))

    @pl.when(third == tiles - 1)
    def _():
        unit, scale = norm_parts(grad_ref[...])
        normed_grad = total[...]
        residual_grad = cot_scr[...].astype(f32) + norm_back(
            normed_grad, unit, scale, gain_ref[...]
        )
        low = residual_grad.astype(bf16)
        grad_ref[...] = residual_grad
        low_scr[...] = low
        att_scr[...] = dot(proj_other_ref[...], low, 1, 1).astype(bf16)
        att_far.start()
        att_grad_ref[...] = dot(proj_ref[...], low, 1, 1).astype(bf16)
        vector_ref[0:1] = column_sum(normed_grad * unit)
        vector_ref[1:2] = column_sum(normed_grad)
        vector_ref[2:3] = column_sum(low.astype(f32))

    fourth = step - 3 * tiles

    @pl.when((fourth >= 0) & (fourth < tiles))
    def _():
        value = dot(n_scr[...], slope_scr[clamp(fourth, tiles - 1)], 0, 0)
        send_gradient(value, keep_ref.at[0])

    @pl.when(fourth == tiles)
    def _():
        send_gradient(dot(low_scr[...], att_ref[...], 0, 1), keep_ref.at[0])

    @pl.when(fourth == tiles + 1)
    def _():
        send_gradient(dot(low_scr[...], att_other_ref[...], 0, 1), keep_ref.at[0])

    @pl.when((second + 1 >= 0) & (second + 1 < tiles))
    def _():
        to_core(second + 1).wait_recv()
        arrive(second + 1).start()

    @pl.when((second >= 0) & (second < tiles))
    def _():
        arrive(second).wait()
        tile = clamp(second, tiles - 1)
        fold(
            keep_ring.at[tile],
            arrived.at[tile % 2],
            x_side,
            keep_x_ref.at[0],
            outgoing_x.at[tile],
        )
        to_x(tile).start()

    @pl.when(step == last)
    def _():
        gather_qkv.wait(2)
        items = got_hbm.shape[0]
        to_core(items - 2).wait_send()
        to_core(items - 1).wait_send()
        for index in range(tiles, items):
            to_core(index).wait_recv()
        for index in range(tiles):
            to_x(index).wait()
        att_far.wait()
        out_near.wait()
        out_far.wait()


def feed_forward(
    count,
    att_mine,
    att_other,
    proj,
    proj_other,
    proj_bias,
    gain,
    shift,
    down_bias,
    up_bias,
    patches,
    cot,
    up,
    up_other,
    down,
    down_part,
    qkv,
):
    tokens, width = patches.shape
    half = tokens // 2
    columns = proj.shape[0]
    tiles = 2 * up.shape[1] // FF_TILE
    items = 2 * tiles + 2
    row = once((1, width))
    left = (width // count, FF_TILE)
    tile = lambda first, lead, size: pl.BlockSpec(
        (1,) + lead, lambda i: (clamp(i - first, size - 1),) + (0,) * len(lead)
    )
    vmem = pltpu.VMEM
    dma = lambda *shape: pltpu.SemaphoreType.DMA(shape)
    return pl.pallas_call(
        feed_kernel,
        grid=(4 * tiles + 2,),
        in_specs=[
            once((columns, half)),
            once((columns, half)),
            once(proj.shape),
            once(proj.shape),
            row,
            row,
            row,
            row,
            once(up_bias.shape),
            HBM,
            HBM,
            HBM,
            HBM,
            HBM,
            HBM,
            HBM,
        ],
        out_specs=(
            once((half, width)),
            once((columns, half)),
            once((columns, half)),
            once((4, width)),
            tile(2 * tiles, (1, FF_TILE), tiles),
            tile(tiles, (count // 4,) + left, tiles),
            tile(3 * tiles, (count // 2,) + left, tiles + 2),
            HBM,
            HBM,
            HBM,
            HBM,
            HBM,
            HBM,
        ),
        out_shape=(
            jax.ShapeDtypeStruct((half, width), f32),
            jax.ShapeDtypeStruct((columns, half), bf16),
            jax.ShapeDtypeStruct((columns, half), bf16),
            jax.ShapeDtypeStruct((4, width), f32),
            jax.ShapeDtypeStruct((tiles, 1, FF_TILE), f32),
            jax.ShapeDtypeStruct((tiles, count // 4) + left, bf16),
            jax.ShapeDtypeStruct((tiles + 2, count // 2) + left, bf16),
            jax.ShapeDtypeStruct((tokens, width), bf16),
            jax.ShapeDtypeStruct((columns, half), bf16),
            jax.ShapeDtypeStruct((items, count // 2) + left, bf16),
            jax.ShapeDtypeStruct((tiles, count // 4) + left, bf16),
            jax.ShapeDtypeStruct(down.shape, bf16),
            jax.ShapeDtypeStruct(qkv.shape, bf16),
        ),
        input_output_aliases={14: 11},
        scratch_shapes=[
            vmem((half, width), bf16),
            vmem((half, width), bf16),
            vmem((half, width), bf16),
            vmem((half, width), f32),
            vmem((tiles, half, FF_TILE), bf16),
            vmem((tiles, half, FF_TILE), bf16),
            vmem((2, width, FF_TILE), bf16),
            vmem((2, FF_TILE, width), bf16),
            vmem((half, width), bf16),
            vmem((width, FF_TILE), f32),
            vmem((tiles, count // 2) + left, bf16),
            vmem((2, count // 2) + left, bf16),
            vmem((2, count // 2) + left, bf16),
            vmem((tiles, count // 4) + left, bf16),
            dma(2),
            dma(2),
            dma(2),
            pltpu.SemaphoreType.DMA,
            dma(2),
            dma(2),
            dma(2),
            dma(items),
            dma(2),
            dma(tiles),
            dma(tiles),
            dma(2, Gather.COPIES),
            dma(2, Gather.COPIES),
        ],
        compiler_params=params(2),
        cost_estimate=pl.CostEstimate(
            flops=12 * half * width * tiles * FF_TILE,
            bytes_accessed=60_000_000,
            transcendentals=half * tiles * FF_TILE,
        ),
        name="feed_forward",
    )(
        att_mine,
        att_other,
        proj,
        proj_other,
        proj_bias[None, :],
        gain[None, :],
        shift[None, :],
        down_bias[None, :],
        up_bias,
        patches,
        cot,
        up,
        up_other,
        down,
        down_part,
        qkv,
    )


class Chain:
    def __init__(self, keep, got, bits, scratch):
        self.keep, self.got, self.bits, self.scratch = keep, got, list(bits), list(scratch)
        self.last = None

    def step(self):
        if self.last is not None:
            self.copy(*self.last).wait()
            self.last = None
        if not self.bits:
            return
        bit = self.bits.pop(0)
        keep, send, got, sem = self.scratch.pop(0)
        fold(self.keep, self.got, partner_of(bit)[1], keep, send)
        self.last = (bit, send, got, sem)
        self.copy(*self.last).start()
        self.keep, self.got = keep, got

    def copy(self, bit, send, got, sem):
        return remote(send, got, sem.at[0], sem.at[1], partner_of(bit)[0])

    def result(self, tile):
        value = self.keep[tile, 0].astype(f32)
        return value if self.got is None else value + self.got[tile, 0].astype(f32)


def input_back_kernel(
    bits,
    mine_ref,
    other_ref,
    w_ref,
    w_other_ref,
    gain_ref,
    vector_ref,
    down_sum,
    up_sum,
    qkv_keep,
    qkv_got,
    x_hbm,
    grad_hbm,
    total_ref,
    down_ref,
    up_ref,
    proj_ref,
    qkv_ref,
    out_hbm,
    total,
    x_scr,
    grad_scr,
    out_scr,
    vector_send,
    vector_got,
    vector_scr,
    vector_next,
    side_send,
    side_got,
    load_sem,
    store_sem,
    row_send,
    row_recv,
    vector_sem,
    side_sem,
    *scratch,
):
    step = pl.program_id(0)
    half, width = total.shape
    side = lax.axis_index("tensor")
    peer = {"tensor": 1 - side}
    mine = pl.ds(pl.multiple_of(side * half, 16), half)
    loads = [
        pltpu.make_async_copy(x_hbm.at[mine], x_scr, load_sem.at[0]),
        pltpu.make_async_copy(grad_hbm, grad_scr, load_sem.at[1]),
    ]
    stages, rest = [], list(scratch)
    for first in (4, 3, 1):
        stages.append([tuple(rest[4 * i : 4 * i + 4]) for i in range(bits - first)])
        rest = rest[4 * (bits - first) :]
    down = Chain(down_sum, None, range(4, bits), stages[0])
    up = Chain(up_sum, None, range(3, bits), stages[1])
    qkv = Chain(qkv_keep, qkv_got, range(1, bits), stages[2])
    tiles = down_ref.shape[1] // FF_TILE
    early_down = not down.bits

    def side_copy(at, size):
        return remote(
            side_send.at[pl.ds(at, size)],
            side_got.at[pl.ds(at, size)],
            side_sem.at[2 * (at // tiles)],
            side_sem.at[2 * (at // tiles) + 1],
            peer,
        )

    def other_side(parts, at):
        for number, part in enumerate(parts):
            side_send[at + number] = part.astype(bf16)
        copy = side_copy(at, len(parts))
        copy.start()
        return copy

    @pl.when(step == 0)
    def _():
        for load in loads:
            load.start()
        greet([peer] + [partner_of(bit)[0] for bit in range(bits)])
        if early_down:
            other_side([down.result(tiles + i) for i in range(tiles)], 0)
        for chain in (up, qkv, down):
            chain.step()

    heads = other_ref.shape[0]
    left = other_ref[...].reshape(heads * HEAD_DIM, half)
    term = dot(mine_ref[0], w_ref[0], 0, 1) + dot(left, w_other_ref[0], 0, 1)
    accumulate(step, total, term)

    @pl.when(step == pl.num_programs(0) - 1)
    def _():
        for load in loads:
            load.wait()
        gain = gain_ref[...]
        sums = [0.0, 0.0]
        begin, blocks = 0, []
        for block, rows in enumerate((half // 32 * 16, half - half // 32 * 16)):
            at = pl.ds(begin, rows)
            unit, scale = norm_parts(x_scr[at].astype(f32))
            normed_grad = total[at]
            out = grad_scr[at] + norm_back(normed_grad, unit, scale, gain)
            out_scr[at] = out.astype(bf16)
            sums = [sums[0] + column_sum(normed_grad * unit), sums[1] + column_sum(normed_grad)]
            target = out_hbm.at[pl.ds(pl.multiple_of(side * half + begin, 16), rows)]
            blocks.append(
                (
                    remote(out_scr.at[at], target, row_send.at[block], row_recv.at[block], peer),
                    pltpu.make_async_copy(out_scr.at[at], target, store_sem.at[block]),
                )
            )
            begin += rows

        both = vector_got.shape[1]
        vector_send[:, : 2 * width] = jnp.concatenate(sums, axis=1)
        vector_send[:, 2 * width :] = vector_ref[1:2, 2 * width : both]
        vector_copy = remote(vector_send, vector_got, vector_sem.at[0], vector_sem.at[1], peer)
        vector_copy.start()
        for far, near in blocks:
            far.start()
            near.start()

        def add_vectors(bit):
            copy = remote(
                vector_scr,
                vector_next.at[bit],
                vector_sem.at[2 * bit + 2],
                vector_sem.at[2 * bit + 3],
                partner_of(bit)[0],
            )
            copy.start()
            copy.wait()
            vector_scr[...] += vector_next[bit]

        qkv.step()
        vector_copy.wait()
        vector_scr[:, :both] = vector_got[...] + jnp.concatenate(
            sums + [vector_ref[0:1, 2 * width : both]], axis=1
        )
        vector_scr[:, both:] = vector_ref[0:1, both:]
        vector_bits = list(range(bits))
        while down.bits or up.bits or qkv.bits:
            if vector_bits:
                add_vectors(vector_bits.pop(0))
            for chain in (qkv, up, down):
                chain.step()
        if early_down:
            down_copy = side_copy(0, tiles)
        else:
            down.step()
            down_copy = other_side([down.result(tiles + i) for i in range(tiles)], 0)
        up.step()
        up_copy = other_side(
            [up.result(tiles + i) for i in range(tiles)] + [up.result(2 * tiles + 1)], tiles
        )
        for bit in vector_bits:
            add_vectors(bit)
        total_ref[...] = vector_scr[...]
        qkv.step()
        for part in range(3):
            qkv_ref[part] = qkv.result(part)
        down_copy.wait()
        for tile in range(tiles):
            at = pl.ds(tile * FF_TILE, FF_TILE)
            down_ref[:, at] = down.result(tile) + side_got[tile].astype(f32)
        up_copy.wait()
        for tile in range(tiles):
            at = pl.ds(tile * FF_TILE, FF_TILE)
            up_ref[:, at] = up.result(tile) + side_got[tiles + tile].astype(f32)
        proj_ref[...] = up.result(2 * tiles) + side_got[2 * tiles].astype(f32)
        for far, near in blocks:
            near.wait()
            far.wait()


def input_backward(
    count,
    mine,
    other,
    weight,
    weight_other,
    gain,
    vectors,
    down_sum,
    up_sum,
    qkv_keep,
    qkv_got,
    patches,
    residual_grad,
):
    tokens, width = patches.shape
    half = tokens // 2
    columns = mine.shape[1]
    heads = other.shape[0]
    bits = count.bit_length() - 1
    rows = width // count
    tiles = heads // 2
    size = vectors.shape[1]
    both = size - FF_TILE * 3
    vmem = pltpu.VMEM
    dma = lambda *shape: pltpu.SemaphoreType.DMA(shape)
    scratch = []
    for first, lead in ((4, heads), (3, heads + 2), (1, 3)):
        for bit in range(first, bits):
            shape = (lead, count >> (bit + 1), rows, FF_TILE)
            scratch += [vmem(shape, bf16), vmem(shape, bf16), vmem(shape, bf16), dma(2)]
    return pl.pallas_call(
        functools.partial(input_back_kernel, bits),
        grid=(3,),
        in_specs=[
            pl.BlockSpec((1, columns, half), lambda i: (i, 0, 0)),
            pl.BlockSpec((heads, None, HEAD_DIM, half), lambda i: (0, i, 0, 0)),
            pl.BlockSpec((1, width, columns), lambda i: (i, 0, 0)),
            pl.BlockSpec((1, width, columns), lambda i: (i, 0, 0)),
            once((1, width)),
            once(vectors.shape),
            once(down_sum.shape),
            once(up_sum.shape),
            once(qkv_keep.shape),
            once(qkv_got.shape),
            HBM,
            HBM,
        ],
        out_specs=(
            once((1, size)),
            once((rows, tiles * FF_TILE)),
            once((rows, tiles * FF_TILE)),
            once((rows, columns)),
            once((3, rows, columns)),
            HBM,
        ),
        out_shape=(
            jax.ShapeDtypeStruct((1, size), f32),
            jax.ShapeDtypeStruct((rows, tiles * FF_TILE), f32),
            jax.ShapeDtypeStruct((rows, tiles * FF_TILE), f32),
            jax.ShapeDtypeStruct((rows, columns), f32),
            jax.ShapeDtypeStruct((3, rows, columns), f32),
            jax.ShapeDtypeStruct((tokens, width), bf16),
        ),
        scratch_shapes=[
            vmem((half, width), f32),
            vmem((half, width), bf16),
            vmem((half, width), f32),
            vmem((half, width), bf16),
            vmem((1, both), f32),
            vmem((1, both), f32),
            vmem((1, size), f32),
            vmem((bits, 1, size), f32),
            vmem((2 * tiles + 1, rows, FF_TILE), bf16),
            vmem((2 * tiles + 1, rows, FF_TILE), bf16),
            dma(2),
            dma(2),
            dma(2),
            dma(2),
            dma(2 * bits + 2),
            dma(4),
        ]
        + scratch,
        compiler_params=params(1),
        cost_estimate=pl.CostEstimate(
            flops=12 * half * width * columns, bytes_accessed=20_000_000, transcendentals=0
        ),
        name="input_backward",
    )(
        mine,
        other,
        weight,
        weight_other,
        gain[None, :],
        vectors,
        down_sum,
        up_sum,
        qkv_keep,
        qkv_got,
        patches,
        residual_grad,
    )


def over_tensor(value):
    return lax.ppermute(value, "tensor", [(0, 1), (1, 0)])


def on_device(
    count,
    patches,
    cotangent,
    clip_lengths,
    attn_gain,
    attn_shift,
    qkv_weight,
    qkv_bias,
    proj_weight,
    proj_bias,
    mlp_gain,
    mlp_shift,
    up_weight,
    up_bias,
    down_weight,
    down_bias,
):
    tokens, width = patches.shape
    local_width = proj_weight.shape[0]

    qkv_parts = jnp.transpose(qkv_weight, (1, 0, 2))
    up_biases = jnp.concatenate([up_bias, over_tensor(up_bias)]).reshape(-1, 1, FF_TILE)

    clip_len = clip_lengths[0, 0]
    cosine, sine = rotary_angles(jnp.arange(tokens, dtype=jnp.int32) % clip_len)
    query_mask, key_mask = clip_masks(clip_len, tokens)
    (
        normed,
        qkv,
        attended,
        att_mine,
        totals,
        weights,
        att_other,
        proj_other,
        up_other,
        down_part,
    ) = attend_forward(
        patches,
        attn_gain,
        attn_shift,
        qkv_parts,
        qkv_bias,
        cosine,
        sine,
        query_mask,
        key_mask,
        proj_weight,
        up_weight,
        down_weight,
    )
    (
        residual_grad,
        att_grad_mine,
        att_grad_send,
        vectors,
        up_bias_grad,
        down_keep,
        up_keep,
        block_out,
        att_grad_got,
        up_got,
        down_got,
        _,
        qkv_other,
    ) = feed_forward(
        count,
        att_mine,
        att_other,
        proj_weight,
        proj_other,
        proj_bias,
        mlp_gain,
        mlp_shift,
        down_bias,
        up_biases,
        patches,
        cotangent,
        up_weight,
        up_other,
        down_weight,
        down_part,
        qkv_parts,
    )
    (
        mixed_mine,
        qkv_keep,
        qkv_bias_grad,
        down_sum,
        up_sum,
        mixed_other,
        qkv_got,
        _,
    ) = attend_backward(
        count,
        weights,
        qkv,
        attended,
        totals,
        att_grad_mine,
        att_grad_send,
        att_grad_got,
        cosine,
        sine,
        normed,
        down_keep,
        down_got,
        up_keep,
        up_got,
    )

    hidden = up_bias.shape[0]
    vectors = vectors.reshape(1, -1)
    up_bias_grad = up_bias_grad.reshape(2, hidden)
    ends = jnp.zeros((2, 2 * width), f32)
    vectors = jnp.concatenate(
        [
            ends,
            jnp.concatenate([vectors, vectors]),
            up_bias_grad,
            jnp.concatenate([qkv_bias_grad.reshape(1, -1)] * 2),
        ],
        axis=1,
    )
    vectors, down_grad, up_grad, proj_grad, qkv_grad, patch_grad = input_backward(
        count,
        mixed_mine,
        mixed_other,
        qkv_parts,
        qkv_other,
        attn_gain,
        vectors,
        down_sum,
        up_sum,
        qkv_keep,
        qkv_got,
        patches,
        residual_grad,
    )
    part = lambda first, size=width: vectors[0, first : first + size]
    return (
        block_out,
        patch_grad,
        part(0),
        part(width),
        jnp.transpose(qkv_grad, (1, 0, 2)),
        part(6 * width + hidden, 3 * local_width).reshape(3, local_width),
        proj_grad.T,
        part(4 * width),
        part(2 * width),
        part(3 * width),
        up_grad,
        part(6 * width, hidden),
        down_grad.T,
        part(5 * width),
    )


def solution(mesh):
    return jax.shard_map(
        functools.partial(on_device, mesh.shape["dp"]),
        mesh=mesh,
        in_specs=(
            P("dp", None),
            P("dp", None),
            P("dp", None),
            P(),
            P(),
            P(None, None, "tensor"),
            P(None, "tensor"),
            P("tensor", None),
            P(),
            P(),
            P(),
            P(None, "tensor"),
            P("tensor"),
            P("tensor", None),
            P(),
        ),
        out_specs=(
            P("dp", None),
            P("dp", None),
            P(),
            P(),
            P("dp", None, "tensor"),
            P(None, "tensor"),
            P("tensor", "dp"),
            P(),
            P(),
            P(),
            P("dp", "tensor"),
            P("tensor"),
            P("tensor", "dp"),
            P(),
        ),
        check_vma=False,
    )
```

profile of v0, /device:TPU:0, one launch (start us, length us, event | category | flops | bytes accessed | tf_op | source)
XLA Modules:
  0.0 337.3 jit_solution(17970284375248272859)
XLA Ops:
  0.6 3.0 collective-permute-start
  5.0 0.1 fusion.6
  5.1 0.1 fusion.8
  6.0 0.6 fusion.2.km_ref
  6.6 0.7 select_convert_fusion.qm_ref
  7.3 1.6 fusion
  8.9 0.0 copy-start.7
  8.9 57.5 %attend_forward.1 = (bf16[1040,1568]{1,0:T(8,128)(2,1)}, bf16[3,512,1568]{2,1,0:T(8,128)(2,1)}, bf16[512,1568]{1,0:T(8,128)(2,1)}, bf16[512,784]{1,0:T(8,128)(2,...) custom-call(bf16[1568,1024]{1,0:T(8,128)(2,1)} %x_hbm.1, ...), custom_call_target="tpu_custom_call" | custom-call | flops 25073549312 | bytes 60000000 | tf_op jit(solution)/shard_map/attend_forward/pallas_call | solution.py:390
  66.4 0.0 collective-permute-done
  66.4 0.0 copy-done.7
  66.5 0.6 pad_maximum_fusion.up_bias_ref
  67.1 113.1 %feed_forward.1 = (f32[784,1024]{1,0:T(8,128)}, bf16[512,784]{1,0:T(8,128)(2,1)}, bf16[512,784]{1,0:T(8,128)(2,1)}, f32[4,1024]{1,0:T(4,128)}, f32[8,1,512]{2,1,...) custom-call(bf16[512,784]{1,0:T(8,128)(2,1)} %get-tuple-element.49.a, ...), custom_call_target="tpu_custom_call", output_to_operand_aliasing={{11}: (14, {})} | custom-call | flops 39460012032 | bytes 60000000 | tf_op jit(solution)/shard_map/feed_forward/pallas_call | solution.py:1168
  180.2 0.0 copy-start.6
  180.2 0.0 copy-start.5
  180.2 83.1 %attend_backward.1 = (bf16[3,512,784]{2,1,0:T(8,128)(2,1)}, bf16[3,8,64,512]{3,2,1,0:T(8,128)(2,1)}, f32[3,512]{1,0:T(4,128)}, f32[8,1,64,512]{3,2,1,0:T(8,128)}...) custom-call(bf16[8,1568,1568]{2,1,0:T(8,128)(2,1)} %get-tuple-elemen, ...), custom_call_target="tpu_custom_call", output_to_operand_aliasing={{7}: (15, {})} | custom-call | flops 40282095616 | bytes 39337984 | tf_op jit(solution)/shard_map/attend_backward/pallas_call | solution.py:723
  263.3 0.7 copy.32
  264.0 0.0 copy-done.6
  264.1 0.0 copy-done.5
  264.1 0.7 maximum_maximum_fusion.vector_ref
  264.8 59.4 %input_backward.1 = (f32[1,9728]{1,0:T(1,128)}, f32[64,2048]{1,0:T(8,128)}, f32[64,2048]{1,0:T(8,128)}, f32[64,512]{1,0:T(8,128)}, f32[3,64,512]{2,1,0:T(8,128)}, /*index=5*/bf16[1568,1024]{1,0:T(8,128)(2,1)}) custom-call(bf16[3,512,784]{2,1,0:T(8,128)(2,1)} %get-tuple-element.67.mine_ref, bf16[8,3,64,784]{3,2,1,0:T(8,128)(2,1)} %get-tuple-element.68.other_ref, ...), custom_call_target="tpu_custom_call" | custom-call | flops 4932501504 | bytes 20000000 | tf_op jit(solution)/shard_map/input_backward/pallas_call | solution.py:1506
  324.2 1.3 fusion.27
  325.5 0.7 slice_reduce_fusion
  326.2 1.3 slice.34
  327.5 0.6 reshape_squeeze.3
  328.1 0.0 copy-start
  328.1 4.1 %copy.41 = bf16[1568,1024]{1,0:T(8,128)(2,1)} copy(bf16[1568,1024]{1,0:T(8,128)(2,1)} %get-tuple-element.110) | data formatting | bytes 6422528
  332.2 0.0 copy-done
  332.2 0.0 copy-start.3
  332.2 0.0 copy-start.4
  332.2 0.0 copy-start.2
  332.2 0.0 copy-start.1
  332.2 1.7 copy.42
  333.9 0.0 copy-done.3
  333.9 0.7 copy.43
  334.6 0.0 copy-done.4
  334.6 0.7 copy.44
  335.3 0.0 copy-done.2
  335.3 0.8 copy.45
  336.1 0.0 copy-done.1
  336.1 0.8 copy.46
  (9 shorter events, 0.1 us)
Async XLA Ops:
  0.6 65.8 %collective-permute-start = (f32[2048]{0:T(1024)}, f32[2048]{0:T(1024)S(1)}, u32[]{:S(2)}, u32[]{:S(2)}) collective-permute-start(f32[2048]{0:T(1024)} %param.27), channel_id=1, source_target_pairs={{0,1},{1,0},{2,3},{3,2},{4,5},{5,4},{6,7},{7,6},{8,9},{9,8},{10,11... | collective-permute-start | bytes 24584 | tf_op jit(solution)/shard_map/ppermute | solution.py:1580
  8.9 57.5 %copy-start.7 = (f32[2048]{0:T(1024)S(1)}, f32[2048]{0:T(1024)}, u32[]{:S(2)}) copy-start(f32[2048]{0:T(1024)} %param.27) | copy-start | bytes 24580
  180.2 83.8 %copy-start.6 = (f32[8,1,512]{2,1,0:T(1,128)S(1)}, f32[8,1,512]{2,1,0:T(1,128)}, u32[]{:S(2)}) copy-start(f32[8,1,512]{2,1,0:T(1,128)} %get-tuple-element.71) | copy-start | bytes 49156
  180.2 83.9 %copy-start.5 = (f32[4,1024]{1,0:T(4,128)S(1)}, f32[4,1024]{1,0:T(4,128)}, u32[]{:S(2)}) copy-start(f32[4,1024]{1,0:T(4,128)} %get-tuple-element.70) | copy-start | bytes 49156
  328.1 4.1 %copy-start = (bf16[1568,1024]{1,0:T(8,128)(2,1)S(1)}, bf16[1568,1024]{1,0:T(8,128)(2,1)}, u32[]{:S(2)}) copy-start(bf16[1568,1024]{1,0:T(8,128)(2,1)} %get-tuple-element.111) | copy-start | bytes 9633796
  332.2 1.7 copy-start.3
  332.2 2.5 copy-start.4
  332.2 3.1 copy-start.2
  332.2 3.9 %copy-start.1 = (f32[64,2048]{1,0:T(8,128)S(1)}, f32[64,2048]{1,0:T(8,128)}, u32[]{:S(2)}) copy-start(f32[64,2048]{1,0:T(8,128)} %get-tuple-element.83) | copy-start | bytes 1572868
where the time goes:
time: 340 us; the launch traced here: 337 us
  Pallas kernels  313 us (92%)
  local copies, waits for them, and re-layouts  13.5 us (4%)
  other arithmetic  4.61 us (1%)
    pallas_call x1, Pallas kernels, feed_forward(): pl.pallas_call(feed_kernel, grid=(4 * tiles + 2,), in_specs=[once((column...  113 us
    pallas_call x1, Pallas kernels, attend_backward(): pl.pallas_call(attend_back_kernel, grid=(heads,), out_shape=(jax.ShapeDty...  83.1 us
    pallas_call x1, Pallas kernels, input_backward(): pl.pallas_call(functools.partial(input_back_kernel, bits), grid=(3,), in_...  59.4 us
    pallas_call x1, Pallas kernels, attend_forward(): pl.pallas_call(attend_kernel, grid=(3 + heads,), out_shape=(jax.ShapeDtyp...  57.5 us
    unnamed x24, local copies, waits for them, and re-layouts  9.5 us
  transfers between devices with their start and end apart: 1, of which 0 were waited for; matrix products, arithmetic and copies ran while one was open for 1% of the time, Pallas kernels for 17%

commit v1 on v0

--- a/solution.py
+++ b/solution.py
@@ -17,6 +17,8 @@
 LOG2E = math.log2(math.e)
 KEY_CHUNKS = 2
 MASK_ROWS = 16
+END_WIDTH = 256
+RESULT_STEPS = 7
 ONES_ROWS = 16
 FF_TILE = 512
 FORBIDDEN = -1e30
@@ -226,6 +228,7 @@
     sin_ref,
     qm_ref,
     km_ref,
+    up_bias_ref,
     proj_hbm,
     up_hbm,
     down_hbm,
@@ -234,6 +237,7 @@
     att_ref,
     mine_ref,
     factor_ref,
+    biases_ref,
     e_hbm,
     other_hbm,
     proj_other,
@@ -243,7 +247,9 @@
     s_scr,
     e_scr,
     outgoing,
+    bias_got,
     e_sem,
+    bias_sem,
     send_sem,
     recv_sem,
     gather_send,
@@ -260,9 +266,12 @@
     up = Gather(up_hbm, up_other, gather_send.at[1], gather_recv.at[1])
     down = Gather(down_hbm, down_other, gather_send.at[2], gather_recv.at[2])
 
+    bias_far = remote(up_bias_ref, bias_got, bias_sem.at[0], bias_sem.at[1], peer)
+
     @pl.when(step == 0)
     def _():
         greet(neighbours())
+        bias_far.start()
         proj.start(0)
         up.start(0)
         unit, _ = norm_parts(x_ref[...].astype(f32))
@@ -373,18 +382,34 @@
                 store(heads - back, part).wait()
         for index in range(heads):
             exchange(index).wait()
+        bias_far.wait()
+        biases_ref[: bias_got.shape[0]] = up_bias_ref[...]
+        biases_ref[bias_got.shape[0] :] = bias_got[...]
         for weight, stage in ((proj, 3), (up, 3), (down, 0)):
             weight.wait(stage)
 
 
 def attend_forward(
-    patches, gain, shift, weight, bias, cosine, sine, query_mask, key_mask, proj, up, down
+    patches,
+    gain,
+    shift,
+    weight,
+    bias,
+    cosine,
+    sine,
+    query_mask,
+    key_mask,
+    up_bias,
+    proj,
+    up,
+    down,
 ):
     tokens, width = patches.shape
     columns = weight.shape[2]
     heads = columns // HEAD_DIM
     half = tokens // 2
     head = lambda i: clamp(i - 3, heads - 1)
+    tiles = up_bias.shape[0] // FF_TILE
     vmem = pltpu.VMEM
     dma = lambda *shape: pltpu.SemaphoreType.DMA(shape)
     return pl.pallas_call(
@@ -396,6 +421,7 @@
             jax.ShapeDtypeStruct((columns, tokens), bf16),
             jax.ShapeDtypeStruct((columns, half), bf16),
             jax.ShapeDtypeStruct((heads, KEY_CHUNKS, tokens), f32),
+            jax.ShapeDtypeStruct((2 * tiles, 1, FF_TILE), f32),
             jax.ShapeDtypeStruct((heads, tokens, tokens), bf16),
             jax.ShapeDtypeStruct((columns, half), bf16),
             jax.ShapeDtypeStruct(proj.shape, bf16),
@@ -412,6 +438,7 @@
             once(sine.shape),
             once(query_mask.shape),
             once(key_mask.shape),
+            once((tiles, 1, FF_TILE)),
             HBM,
             HBM,
             HBM,
@@ -422,6 +449,7 @@
             pl.BlockSpec((HEAD_DIM, tokens), lambda i: (head(i), 0)),
             pl.BlockSpec((HEAD_DIM, half), lambda i: (head(i), 0)),
             pl.BlockSpec((1, KEY_CHUNKS, tokens), lambda i: (head(i), 0, 0)),
+            once((2 * tiles, 1, FF_TILE)),
             HBM,
             HBM,
             HBM,
@@ -433,7 +461,9 @@
             vmem((2, tokens // KEY_CHUNKS, tokens), f32),
             vmem((2, tokens, tokens), bf16),
             vmem((heads, HEAD_DIM, half), bf16),
+            vmem((tiles, 1, FF_TILE), f32),
             dma(2, KEY_CHUNKS),
+            dma(2),
             dma(heads),
             dma(heads),
             dma(3, Gather.COPIES),
@@ -456,6 +486,7 @@
         sine,
         query_mask,
         key_mask,
+        up_bias.reshape(tiles, 1, FF_TILE),
         proj,
         up,
         down,
@@ -484,7 +515,9 @@
     sum_ref,
     down_sum_ref,
     up_sum_ref,
+    proj_sum_ref,
     other_ref,
+    other_end_ref,
     got_ref,
     att_got_hbm,
     att_scr,
@@ -496,6 +529,7 @@
     turned,
     pair_scr,
     outgoing,
+    outgoing_end,
     grad,
     outgoing_core,
     down_scr,
@@ -504,6 +538,7 @@
     up_last,
     send_sem,
     recv_sem,
+    end_sem,
     core_send,
     core_recv,
     down_sem,
@@ -529,6 +564,10 @@
             peer,
         )
 
+    end_far = remote(outgoing_end, other_end_ref, end_sem.at[0], end_sem.at[1], peer)
+    lanes = half // 128 * 128
+    end_width = outgoing_end.shape[1] // heads
+
     def to_core(pair):
         at = pl.ds(pl.multiple_of(pair * 2 * HEAD_DIM, 2 * HEAD_DIM), 2 * HEAD_DIM)
         return remote(
@@ -559,7 +598,7 @@
         at = pl.ds(2 * pair, 2)
         start(source.at[0, at], source.at[2, at], buffers, sems, pair, bit)
 
-    down_pairs, up_pairs = down_scr.shape[1] // 2, up_first.shape[1] // 2
+    down_pairs, up_pairs = down_scr.shape[1] // 2, up_last.shape[1] // 2
     behind = heads - up_pairs
 
     late_heads = pl.ds(att_got_hbm.shape[0] // 2, att_got_hbm.shape[0] // 2)
@@ -583,7 +622,7 @@
     def _():
         exchange(head - 4).wait_send()
 
-    @pl.when(head < up_pairs)
+    @pl.when(head <= up_pairs)
     def _():
         start(up_keep_ref, up_got_ref, up_first, up_sem, head, 1)
 
@@ -623,13 +662,15 @@
     v_scr[...] = v_ref[0].T
     cosine, sine = cos_ref[...], sin_ref[...]
 
+    ends = {}
+
     def store(part, low, high):
         for row, value in ((0, low), (HALF_DIM, high)):
             left, right = value[:, :half], value[:, half:]
             mine_ref[part, row : row + HALF_DIM] = jnp.where(side == 0, left, right).astype(bf16)
-            outgoing[head % 4, part, row : row + HALF_DIM] = jnp.where(
-                side == 0, right, left
-            ).astype(bf16)
+            theirs = jnp.where(side == 0, right, left)
+            outgoing[head % 4, part, row : row + HALF_DIM] = theirs[:, :lanes].astype(bf16)
+            ends[part, row // HALF_DIM] = theirs[:, lanes:]
             begin = pl.multiple_of(part * 2 * HEAD_DIM + slot * HEAD_DIM + row, HALF_DIM)
             pair_scr[pl.ds(begin, HALF_DIM)] = value.astype(bf16)
 
@@ -647,6 +688,10 @@
     turned[...] = score_grad[...].T
     unrotated(1, dot(q_ref[0], turned[...], 1, 0))
     exchange(head).start()
+    end = jnp.concatenate([ends[part, row] for part in range(3) for row in range(2)], axis=0)
+    end = jnp.concatenate([end, jnp.zeros((end_width - end.shape[0], end.shape[1]), f32)], axis=0)
+    begin = pl.multiple_of(head * end_width, end_width)
+    outgoing_end[:, pl.ds(begin, end_width)] = end.T.astype(bf16)
 
     @pl.when(slot == 1)
     def _():
@@ -668,6 +713,7 @@
 
     @pl.when(head == heads - 1)
     def _():
+        end_far.start()
         for back in range(4):
             exchange(heads - 1 - back).wait_send()
         for back in range(2):
@@ -682,7 +728,11 @@
             hop(up_first, up_sem, pair, 1).wait_send()
             hop(up_last, up_last_sem, pair, 2).wait()
         up_sum_ref[...] = (up_last[0].astype(f32) + up_last[2].astype(f32)).astype(bf16)
+        hop(up_first, up_sem, up_pairs, 1).wait()
+        at = pl.ds(2 * up_pairs, 2)
+        proj_sum_ref[...] = (up_first[0, at].astype(f32) + up_first[2, at].astype(f32)).astype(bf16)
         att_far.wait_send()
+        end_far.wait()
         for index in range(other_ref.shape[0]):
             exchange(index).wait_recv()
 
@@ -717,6 +767,7 @@
     )
     block = lambda part: pl.BlockSpec((1, HEAD_DIM, tokens), lambda i: (part, i, 0))
     half_block = pl.BlockSpec((HEAD_DIM, half), lambda i: (i, 0))
+    lanes = half // 128 * 128
     pair_block = pl.BlockSpec(split + (2 * HEAD_DIM,), lambda i: (0, 0, 0, i // 2))
     vmem = pltpu.VMEM
     dma = lambda *shape: pltpu.SemaphoreType.DMA(shape)
@@ -728,12 +779,14 @@
             jax.ShapeDtypeStruct(split + (columns,), bf16),
             jax.ShapeDtypeStruct((3, columns), f32),
             jax.ShapeDtypeStruct((heads,) + blocks(4), f32),
-            jax.ShapeDtypeStruct((heads + 2,) + blocks(3), bf16),
-            jax.ShapeDtypeStruct((heads, 3, HEAD_DIM, half), bf16),
+            jax.ShapeDtypeStruct((heads,) + blocks(3), bf16),
+            jax.ShapeDtypeStruct((2,) + blocks(2), bf16),
+            jax.ShapeDtypeStruct((heads, 3, HEAD_DIM, lanes), bf16),
+            jax.ShapeDtypeStruct((half - lanes, heads * END_WIDTH), bf16),
             jax.ShapeDtypeStruct(split + (columns,), bf16),
             jax.ShapeDtypeStruct(att_got.shape, bf16),
         ),
-        input_output_aliases={15: 7},
+        input_output_aliases={15: 9},
         in_specs=[
             pl.BlockSpec((1, tokens, tokens), lambda i: (i, 0, 0)),
             block(0),
@@ -757,7 +810,9 @@
             pair_block,
             pl.BlockSpec((3, 2 * HEAD_DIM), lambda i: (0, i // 2)),
             once((heads,) + blocks(4)),
-            once((heads + 2,) + blocks(3)),
+            once((heads,) + blocks(3)),
+            once((2,) + blocks(2)),
+            HBM,
             HBM,
             HBM,
             HBM,
@@ -771,21 +826,23 @@
             vmem((tokens, tokens), bf16),
             vmem((tokens, tokens), bf16),
             vmem((6 * HEAD_DIM, tokens), bf16),
-            vmem((4, 3, HEAD_DIM, half), bf16),
+            vmem((4, 3, HEAD_DIM, lanes), bf16),
+            vmem((half - lanes, heads * END_WIDTH), bf16),
             vmem((width + ONES_ROWS, 6 * HEAD_DIM), f32),
             vmem((2,) + split + (2 * HEAD_DIM,), bf16),
             vmem((3, heads) + blocks(3), bf16),
             vmem((3, heads) + blocks(4), bf16),
             vmem((3, heads + 2) + blocks(2), bf16),
-            vmem((3, heads + 2) + blocks(3), bf16),
+            vmem((3, heads) + blocks(3), bf16),
             dma(4),
             dma(heads),
+            dma(2),
             dma(2),
             dma(heads // 2),
             dma(2, heads // 2),
             dma(2, heads // 2),
             dma(2, heads // 2 + 1),
-            dma(2, heads // 2 + 1),
+            dma(2, heads // 2),
             dma(2),
             dma(2),
         ],
@@ -1122,7 +1179,7 @@
     @pl.when(step == last)
     def _():
         gather_qkv.wait(2)
-        items = got_hbm.shape[0]
+        items = got_hbm.shape[0] - 1
         to_core(items - 2).wait_send()
         to_core(items - 1).wait_send()
         for index in range(tiles, items):
@@ -1211,7 +1268,7 @@
             jax.ShapeDtypeStruct((tiles + 2, count // 2) + left, bf16),
             jax.ShapeDtypeStruct((tokens, width), bf16),
             jax.ShapeDtypeStruct((columns, half), bf16),
-            jax.ShapeDtypeStruct((items, count // 2) + left, bf16),
+            jax.ShapeDtypeStruct((items + 1, count // 2) + left, bf16),
             jax.ShapeDtypeStruct((tiles, count // 4) + left, bf16),
             jax.ShapeDtypeStruct(down.shape, bf16),
             jax.ShapeDtypeStruct(qkv.shape, bf16),
@@ -1291,6 +1348,11 @@
         self.copy(*self.last).start()
         self.keep, self.got = keep, got
 
+    def finish(self):
+        while self.bits:
+            self.step()
+        self.step()
+
     def copy(self, bit, send, got, sem):
         return remote(send, got, sem.at[0], sem.at[1], partner_of(bit)[0])
 
@@ -1303,12 +1365,14 @@
     bits,
     mine_ref,
     other_ref,
+    other_end_ref,
     w_ref,
     w_other_ref,
     gain_ref,
     vector_ref,
     down_sum,
     up_sum,
+    proj_sum,
     qkv_keep,
     qkv_got,
     x_hbm,
@@ -1338,7 +1402,7 @@
     *scratch,
 ):
     step = pl.program_id(0)
-    half, width = total.shape
+    half, width = grad_scr.shape
     side = lax.axis_index("tensor")
     peer = {"tensor": 1 - side}
     mine = pl.ds(pl.multiple_of(side * half, 16), half)
@@ -1347,12 +1411,13 @@
         pltpu.make_async_copy(grad_hbm, grad_scr, load_sem.at[1]),
     ]
     stages, rest = [], list(scratch)
-    for first in (4, 3, 1):
+    for first in (4, 3, 2, 1):
         stages.append([tuple(rest[4 * i : 4 * i + 4]) for i in range(bits - first)])
         rest = rest[4 * (bits - first) :]
     down = Chain(down_sum, None, range(4, bits), stages[0])
     up = Chain(up_sum, None, range(3, bits), stages[1])
-    qkv = Chain(qkv_keep, qkv_got, range(1, bits), stages[2])
+    proj = Chain(proj_sum, None, range(2, bits), stages[2])
+    qkv = Chain(qkv_keep, qkv_got, range(1, bits), stages[3])
     tiles = down_ref.shape[1] // FF_TILE
     early_down = not down.bits
 
@@ -1368,9 +1433,7 @@
     def other_side(parts, at):
         for number, part in enumerate(parts):
             side_send[at + number] = part.astype(bf16)
-        copy = side_copy(at, len(parts))
-        copy.start()
-        return copy
+        side_copy(at, len(parts)).start()
 
     @pl.when(step == 0)
     def _():
@@ -1379,47 +1442,79 @@
         greet([peer] + [partner_of(bit)[0] for bit in range(bits)])
         if early_down:
             other_side([down.result(tiles + i) for i in range(tiles)], 0)
-        for chain in (up, qkv, down):
+        for chain in (qkv, up, proj, down):
             chain.step()
 
     heads = other_ref.shape[0]
-    left = other_ref[...].reshape(heads * HEAD_DIM, half)
-    term = dot(mine_ref[0], w_ref[0], 0, 1) + dot(left, w_other_ref[0], 0, 1)
-    accumulate(step, total, term)
-
-    @pl.when(step == pl.num_programs(0) - 1)
+    lanes = other_ref.shape[3]
+    gain = gain_ref[...]
+    first_rows = lanes // 256 * 128
+    blocks = ((0, first_rows), (first_rows, half))
+
+    def rows_copies(block):
+        begin, end = blocks[block]
+        at = pl.ds(begin, end - begin)
+        target = out_hbm.at[pl.ds(pl.multiple_of(side * half + begin, 16), end - begin)]
+        return (
+            remote(out_scr.at[at], target, row_send.at[block], row_recv.at[block], peer),
+            pltpu.make_async_copy(out_scr.at[at], target, store_sem.at[block]),
+        )
+
+    def input_rows(block):
+        begin, end = blocks[block]
+        whole_end = min(end, lanes)
+        near, far = 0.0, 0.0
+        for part in range(3):
+            near = near + dot(mine_ref[part, :, begin:end], w_ref[part], 0, 1)
+            left = other_ref[:, part, :, begin:whole_end].reshape(
+                heads * HEAD_DIM, whole_end - begin
+            )
+            far = far + dot(left, w_other_ref[part], 0, 1)
+        if end > lanes:
+            rest = 0.0
+            for part in range(3):
+                ends = [
+                    other_end_ref[:, pl.ds(head * END_WIDTH, 3 * HEAD_DIM)][
+                        :, part * HEAD_DIM : (part + 1) * HEAD_DIM
+                    ]
+                    for head in range(heads)
+                ]
+                rest = rest + dot(jnp.concatenate(ends, axis=1), w_other_ref[part], 1, 1)
+            far = jnp.concatenate([far, rest], axis=0)
+        normed_grad = near + far
+        unit, scale = norm_parts(x_scr[begin:end].astype(f32))
+        out = grad_scr[begin:end] + norm_back(normed_grad, unit, scale, gain)
+        out_scr[begin:end] = out.astype(bf16)
+        return column_sum(normed_grad * unit), column_sum(normed_grad)
+
+    @pl.when(step == 0)
     def _():
         for load in loads:
             load.wait()
-        gain = gain_ref[...]
-        sums = [0.0, 0.0]
-        begin, blocks = 0, []
-        for block, rows in enumerate((half // 32 * 16, half - half // 32 * 16)):
-            at = pl.ds(begin, rows)
-            unit, scale = norm_parts(x_scr[at].astype(f32))
-            normed_grad = total[at]
-            out = grad_scr[at] + norm_back(normed_grad, unit, scale, gain)
-            out_scr[at] = out.astype(bf16)
-            sums = [sums[0] + column_sum(normed_grad * unit), sums[1] + column_sum(normed_grad)]
-            target = out_hbm.at[pl.ds(pl.multiple_of(side * half + begin, 16), rows)]
-            blocks.append(
-                (
-                    remote(out_scr.at[at], target, row_send.at[block], row_recv.at[block], peer),
-                    pltpu.make_async_copy(out_scr.at[at], target, store_sem.at[block]),
-                )
-            )
-            begin += rows
+        sums = input_rows(0)
+        for copy in rows_copies(0):
+            copy.start()
+        total[0:1], total[1:2] = sums
+
+    @pl.when(step == 1)
+    def _():
+        sums = input_rows(1)
+        sums = [total[number : number + 1] + sums[number] for number in range(2)]
 
         both = vector_got.shape[1]
         vector_send[:, : 2 * width] = jnp.concatenate(sums, axis=1)
         vector_send[:, 2 * width :] = vector_ref[1:2, 2 * width : both]
         vector_copy = remote(vector_send, vector_got, vector_sem.at[0], vector_sem.at[1], peer)
         vector_copy.start()
-        for far, near in blocks:
-            far.start()
-            near.start()
-
-        def add_vectors(bit):
+        for copy in rows_copies(1):
+            copy.start()
+
+        vector_bits = list(range(bits))
+
+        def add_vectors():
+            if not vector_bits:
+                return
+            bit = vector_bits.pop(0)
             copy = remote(
                 vector_scr,
                 vector_next.at[bit],
@@ -1432,42 +1527,42 @@
             vector_scr[...] += vector_next[bit]
 
         qkv.step()
+        while proj.bits:
+            proj.step()
         vector_copy.wait()
         vector_scr[:, :both] = vector_got[...] + jnp.concatenate(
             sums + [vector_ref[0:1, 2 * width : both]], axis=1
         )
         vector_scr[:, both:] = vector_ref[0:1, both:]
-        vector_bits = list(range(bits))
-        while down.bits or up.bits or qkv.bits:
-            if vector_bits:
-                add_vectors(vector_bits.pop(0))
-            for chain in (qkv, up, down):
-                chain.step()
-        if early_down:
-            down_copy = side_copy(0, tiles)
-        else:
-            down.step()
-            down_copy = other_side([down.result(tiles + i) for i in range(tiles)], 0)
-        up.step()
-        up_copy = other_side(
-            [up.result(tiles + i) for i in range(tiles)] + [up.result(2 * tiles + 1)], tiles
-        )
-        for bit in vector_bits:
-            add_vectors(bit)
-        total_ref[...] = vector_scr[...]
+        add_vectors()
+        if not early_down:
+            down.finish()
+            other_side([down.result(tiles + i) for i in range(tiles)], 0)
+        up.finish()
+        other_side([up.result(tiles + i) for i in range(tiles)], tiles)
+        add_vectors()
         qkv.step()
-        for part in range(3):
-            qkv_ref[part] = qkv.result(part)
-        down_copy.wait()
+        proj.step()
+        other_side([proj.result(1)], 2 * tiles)
+        add_vectors()
+        side_copy(0, tiles).wait()
         for tile in range(tiles):
             at = pl.ds(tile * FF_TILE, FF_TILE)
             down_ref[:, at] = down.result(tile) + side_got[tile].astype(f32)
-        up_copy.wait()
+        qkv.finish()
+        for part in range(3):
+            qkv_ref[part] = qkv.result(part)
+        while vector_bits:
+            add_vectors()
+        total_ref[...] = vector_scr[...]
+        side_copy(tiles, tiles).wait()
         for tile in range(tiles):
             at = pl.ds(tile * FF_TILE, FF_TILE)
             up_ref[:, at] = up.result(tile) + side_got[tiles + tile].astype(f32)
-        proj_ref[...] = up.result(2 * tiles) + side_got[2 * tiles].astype(f32)
-        for far, near in blocks:
+        side_copy(2 * tiles, 1).wait()
+        proj_ref[...] = proj.result(0) + side_got[2 * tiles].astype(f32)
+        for block in range(2):
+            far, near = rows_copies(block)
             near.wait()
             far.wait()
 
@@ -1476,12 +1571,14 @@
     count,
     mine,
     other,
+    other_end,
     weight,
     weight_other,
     gain,
     vectors,
     down_sum,
     up_sum,
+    proj_sum,
     qkv_keep,
     qkv_got,
     patches,
@@ -1499,22 +1596,24 @@
     vmem = pltpu.VMEM
     dma = lambda *shape: pltpu.SemaphoreType.DMA(shape)
     scratch = []
-    for first, lead in ((4, heads), (3, heads + 2), (1, 3)):
+    for first, lead in ((4, heads), (3, heads), (2, 2), (1, 3)):
         for bit in range(first, bits):
             shape = (lead, count >> (bit + 1), rows, FF_TILE)
             scratch += [vmem(shape, bf16), vmem(shape, bf16), vmem(shape, bf16), dma(2)]
     return pl.pallas_call(
         functools.partial(input_back_kernel, bits),
-        grid=(3,),
+        grid=(2,),
         in_specs=[
-            pl.BlockSpec((1, columns, half), lambda i: (i, 0, 0)),
-            pl.BlockSpec((heads, None, HEAD_DIM, half), lambda i: (0, i, 0, 0)),
-            pl.BlockSpec((1, width, columns), lambda i: (i, 0, 0)),
-            pl.BlockSpec((1, width, columns), lambda i: (i, 0, 0)),
+            once(mine.shape),
+            once(other.shape),
+            once(other_end.shape),
+            once(weight.shape),
+            once(weight_other.shape),
             once((1, width)),
             once(vectors.shape),
             once(down_sum.shape),
             once(up_sum.shape),
+            once(proj_sum.shape),
             once(qkv_keep.shape),
             once(qkv_got.shape),
             HBM,
@@ -1537,7 +1636,7 @@
             jax.ShapeDtypeStruct((tokens, width), bf16),
         ),
         scratch_shapes=[
-            vmem((half, width), f32),
+            vmem((2, width), f32),
             vmem((half, width), bf16),
             vmem((half, width), f32),
             vmem((half, width), bf16),
@@ -1552,7 +1651,7 @@
             dma(2),
             dma(2),
             dma(2 * bits + 2),
-            dma(4),
+            dma(6),
         ]
         + scratch,
         compiler_params=params(1),
@@ -1563,12 +1662,14 @@
     )(
         mine,
         other,
+        other_end,
         weight,
         weight_other,
         gain[None, :],
         vectors,
         down_sum,
         up_sum,
+        proj_sum,
         qkv_keep,
         qkv_got,
         patches,
@@ -1576,8 +1677,41 @@
     )
 
 
-def over_tensor(value):
-    return lax.ppermute(value, "tensor", [(0, 1), (1, 0)])
+def result_kernel(sizes, vector_ref, *refs):
+    count = (len(refs) - len(sizes)) // 2
+    sources, targets = refs[:count], refs[count : 2 * count]
+    for source, target in zip(sources[-2:], targets[-2:]):
+        target[...] = source[...]
+
+    @pl.when(pl.program_id(0) == 0)
+    def _():
+        for source, target in zip(sources[:-2], targets[:-2]):
+            target[...] = source[...]
+        begin = 0
+        for size, target in zip(sizes, refs[2 * count :]):
+            for row in range(size // 128):
+                at = pl.ds(begin + row * 128, 128)
+                target[row : row + 1, :] = vector_ref[:, at]
+            begin += size
+
+
+def results(vectors, sizes, arrays, rows):
+    step = rows[0].shape[0] // RESULT_STEPS
+    long_block = pl.BlockSpec((step, rows[0].shape[1]), lambda i: (i, 0))
+    specs = [once(x.shape) for x in arrays] + [long_block] * len(rows)
+    shapes = [(size // 128, 128) for size in sizes]
+    out = pl.pallas_call(
+        functools.partial(result_kernel, sizes),
+        grid=(RESULT_STEPS,),
+        in_specs=[once(vectors.shape)] + specs,
+        out_specs=specs + [once(x) for x in shapes],
+        out_shape=[jax.ShapeDtypeStruct(x.shape, x.dtype) for x in list(arrays) + list(rows)]
+        + [jax.ShapeDtypeStruct(x, f32) for x in shapes],
+        compiler_params=params(),
+        name="results",
+    )(vectors, *arrays, *rows)
+    count = len(arrays) + len(rows)
+    return out[:count], [x.reshape(-1) for x in out[count:]]
 
 
 def on_device(
@@ -1602,7 +1736,6 @@
     local_width = proj_weight.shape[0]
 
     qkv_parts = jnp.transpose(qkv_weight, (1, 0, 2))
-    up_biases = jnp.concatenate([up_bias, over_tensor(up_bias)]).reshape(-1, 1, FF_TILE)
 
     clip_len = clip_lengths[0, 0]
     cosine, sine = rotary_angles(jnp.arange(tokens, dtype=jnp.int32) % clip_len)
@@ -1613,6 +1746,7 @@
         attended,
         att_mine,
         totals,
+        up_biases,
         weights,
         att_other,
         proj_other,
@@ -1628,6 +1762,7 @@
         sine,
         query_mask,
         key_mask,
+        up_bias,
         proj_weight,
         up_weight,
         down_weight,
@@ -1671,7 +1806,9 @@
         qkv_bias_grad,
         down_sum,
         up_sum,
+        proj_sum,
         mixed_other,
+        mixed_end,
         qkv_got,
         _,
     ) = attend_backward(
@@ -1709,33 +1846,40 @@
         count,
         mixed_mine,
         mixed_other,
+        mixed_end,
         qkv_parts,
         qkv_other,
         attn_gain,
         vectors,
         down_sum,
         up_sum,
+        proj_sum,
         qkv_keep,
         qkv_got,
         patches,
         residual_grad,
     )
-    part = lambda first, size=width: vectors[0, first : first + size]
+    sizes = [width] * 6 + [hidden, 3 * local_width]
+    (down_grad, up_grad, proj_grad, qkv_grad, block_out, patch_grad), pieces = results(
+        vectors, sizes, [down_grad, up_grad, proj_grad, qkv_grad], [block_out, patch_grad]
+    )
+    attn_gain_grad, attn_shift_grad, mlp_gain_grad, mlp_shift_grad = pieces[:4]
+    proj_bias_grad, down_bias_grad, up_bias_grad, qkv_bias_grad = pieces[4:]
     return (
         block_out,
         patch_grad,
-        part(0),
-        part(width),
+        attn_gain_grad,
+        attn_shift_grad,
         jnp.transpose(qkv_grad, (1, 0, 2)),
-        part(6 * width + hidden, 3 * local_width).reshape(3, local_width),
+        qkv_bias_grad.reshape(3, local_width),
         proj_grad.T,
-        part(4 * width),
-        part(2 * width),
-        part(3 * width),
+        proj_bias_grad,
+        mlp_gain_grad,
+        mlp_shift_grad,
         up_grad,
-        part(6 * width, hidden),
+        up_bias_grad,
         down_grad.T,
-        part(5 * width),
+        down_bias_grad,
     )
 
 

time: 340 us -> 327 us (0.962)
  local copies, waits for them, and re-layouts: 13.5 us -> 2.06 us
    pallas_call x1 -> x2, Pallas kernels: 59.4 us -> 68.6 us  [the longest x1 59.4 us: input_backward(): pl.pallas_call(functools.partial(input_back_kernel, bits), grid=(2,), in_...]
    pallas_call x1, Pallas kernels: 83.1 us -> 74.1 us  [attend_backward(): pl.pallas_call(attend_back_kernel, grid=(heads,), out_shape=(jax.ShapeDty...]
    unnamed x24 -> x6, local copies, waits for them, and re-layouts: 9.5 us -> 0.73 us
  transfers between devices with their start and end apart: 1 -> 0, of which waited for: 0 -> 0; matrix products, arithmetic and copies ran while one was open for 1% -> 0% of each run, Pallas kernels for 17% -> 0%
where the time goes in v1:
time: 327 us; the launch traced here: 325 us
  Pallas kernels  315 us (96%)
  other arithmetic  4 us (1%)
    pallas_call x1, Pallas kernels, feed_forward(): pl.pallas_call(feed_kernel, grid=(4 * tiles + 2,), in_specs=[once((column...  112 us
    pallas_call x1, Pallas kernels, attend_backward(): pl.pallas_call(attend_back_kernel, grid=(heads,), out_shape=(jax.ShapeDty...  74.1 us
    pallas_call x1, Pallas kernels, attend_forward(): pl.pallas_call(attend_kernel, grid=(3 + heads,), out_shape=(jax.ShapeDtyp...  60.3 us
    pallas_call x1, Pallas kernels, input_backward(): pl.pallas_call(functools.partial(input_back_kernel, bits), grid=(2,), in_...  59.4 us
    pallas_call x1, Pallas kernels, results(): pl.pallas_call(functools.partial(result_kernel, sizes), grid=(RESULT_STEP...  9.15 us

profile of v1, /device:TPU:0, one launch (start us, length us, event | category | flops | bytes accessed | tf_op | source)
XLA Modules:
  0.0 324.6 jit_solution(17931956357250306441)
XLA Ops:
  1.9 0.1 fusion.6
  2.1 0.1 fusion.8
  2.3 1.6 fusion
  4.6 0.7 select_convert_fusion.qm_ref
  5.3 0.6 fusion.2.km_ref
  5.9 60.3 %attend_forward.1 = (bf16[1040,1568]{1,0:T(8,128)(2,1)}, bf16[3,512,1568]{2,1,0:T(8,128)(2,1)}, bf16[512,1568]{1,0:T(8,128)(2,1)}, bf16[512,784]{1,0:T(8,128)(2,...) custom-call(bf16[1568,1024]{1,0:T(8,128)(2,1)} %x_hbm.1, ...), custom_call_target="tpu_custom_call" | custom-call | flops 25073549312 | bytes 60000000 | tf_op jit(solution)/shard_map/attend_forward/pallas_call | solution.py:415
  66.2 112.4 %feed_forward.1 = (f32[784,1024]{1,0:T(8,128)}, bf16[512,784]{1,0:T(8,128)(2,1)}, bf16[512,784]{1,0:T(8,128)(2,1)}, f32[4,1024]{1,0:T(4,128)}, f32[8,1,512]{2,1,...) custom-call(bf16[512,784]{1,0:T(8,128)(2,1)} %get-tuple-element.70.a, ...), custom_call_target="tpu_custom_call", output_to_operand_aliasing={{11}: (14, {})} | custom-call | flops 39460012032 | bytes 60000000 | tf_op jit(solution)/shard_map/feed_forward/pallas_call | solution.py:1225
  178.6 0.0 copy-start.1
  178.6 0.0 copy-start
  178.6 74.1 %attend_backward.1 = (bf16[3,512,784]{2,1,0:T(8,128)(2,1)}, bf16[3,8,64,512]{3,2,1,0:T(8,128)(2,1)}, f32[3,512]{1,0:T(4,128)}, f32[8,1,64,512]{3,2,1,0:T(8,128)}...) custom-call(bf16[8,1568,1568]{2,1,0:T(8,128)(2,1)} %get-tuple-elemen, ...), custom_call_target="tpu_custom_call", output_to_operand_aliasing={{9}: (15, {})} | custom-call | flops 40282095616 | bytes 39337984 | tf_op jit(solution)/shard_map/attend_backward/pallas_call | solution.py:774
  252.7 0.7 copy.32
  253.4 0.0 copy-done.1
  253.5 0.0 copy-done
  253.6 0.7 maximum_maximum_fusion.vector_ref
  254.3 59.4 %input_backward.1 = (f32[1,9728]{1,0:T(1,128)}, f32[64,2048]{1,0:T(8,128)}, f32[64,2048]{1,0:T(8,128)}, f32[64,512]{1,0:T(8,128)}, f32[3,64,512]{2,1,0:T(8,128)}, /*index=5*/bf16[1568,1024]{1,0:T(8,128)(2,1)}) custom-call(bf16[3,512,784]{2,1,0:T(8,128)(2,1)} %get-tuple-element.84.mine_ref, bf16[8,3,64,768]{3,2,1,0:T(8,128)(2,1)} %get-tuple-element.85.other_ref, ...), custom_call_target="tpu_custom_call" | custom-call | flops 4932501504 | bytes 20000000 | tf_op jit(solution)/shard_map/input_backward/pallas_call | solution.py:1603
  313.7 9.1 %results.1 = (f32[64,2048]{1,0:T(8,128)}, f32[64,2048]{1,0:T(8,128)}, f32[64,512]{1,0:T(8,128)}, f32[3,64,512]{2,1,0:T(8,128)}, bf16[1568,1024]{1,0:T(8,128)(2,1...) custom-call(f32[1,9728]{1,0:T(1,128)} %get-tuple-element.97.vector_r, ...), custom_call_target="tpu_custom_call" | custom-call | tf_op jit(solution)/shard_map/results/pallas_call | solution.py:1703
  322.8 1.3 reshape_reshape.3
  (9 shorter events, 0.1 us)
Async XLA Ops:
  178.6 74.8 %copy-start.1 = (f32[8,1,512]{2,1,0:T(1,128)S(1)}, f32[8,1,512]{2,1,0:T(1,128)}, u32[]{:S(2)}) copy-start(f32[8,1,512]{2,1,0:T(1,128)} %get-tuple-element.89) | copy-start | bytes 49156
  178.6 74.9 %copy-start = (f32[4,1024]{1,0:T(4,128)S(1)}, f32[4,1024]{1,0:T(4,128)}, u32[]{:S(2)}) copy-start(f32[4,1024]{1,0:T(4,128)} %get-tuple-element.88) | copy-start | bytes 49156

commit v2 on v1

--- a/solution.py
+++ b/solution.py
@@ -18,7 +18,7 @@
 KEY_CHUNKS = 2
 MASK_ROWS = 16
 END_WIDTH = 256
-RESULT_STEPS = 7
+RESULT_STEPS = 2
 ONES_ROWS = 16
 FF_TILE = 512
 FORBIDDEN = -1e30
@@ -1363,11 +1363,7 @@
 
 def input_back_kernel(
     bits,
-    mine_ref,
-    other_ref,
     other_end_ref,
-    w_ref,
-    w_other_ref,
     gain_ref,
     vector_ref,
     down_sum,
@@ -1375,6 +1371,10 @@
     proj_sum,
     qkv_keep,
     qkv_got,
+    mine_hbm,
+    other_hbm,
+    w_hbm,
+    w_other_hbm,
     x_hbm,
     grad_hbm,
     total_ref,
@@ -1384,6 +1384,10 @@
     qkv_ref,
     out_hbm,
     total,
+    mine_ref,
+    other_ref,
+    w_ref,
+    w_other_ref,
     x_scr,
     grad_scr,
     out_scr,
@@ -1409,6 +1413,10 @@
     loads = [
         pltpu.make_async_copy(x_hbm.at[mine], x_scr, load_sem.at[0]),
         pltpu.make_async_copy(grad_hbm, grad_scr, load_sem.at[1]),
+        pltpu.make_async_copy(w_hbm, w_ref, load_sem.at[2]),
+        pltpu.make_async_copy(mine_hbm, mine_ref, load_sem.at[3]),
+        pltpu.make_async_copy(w_other_hbm, w_other_ref, load_sem.at[4]),
+        pltpu.make_async_copy(other_hbm, other_ref, load_sem.at[5]),
     ]
     stages, rest = [], list(scratch)
     for first in (4, 3, 2, 1):
@@ -1604,11 +1612,7 @@
         functools.partial(input_back_kernel, bits),
         grid=(2,),
         in_specs=[
-            once(mine.shape),
-            once(other.shape),
             once(other_end.shape),
-            once(weight.shape),
-            once(weight_other.shape),
             once((1, width)),
             once(vectors.shape),
             once(down_sum.shape),
@@ -1616,6 +1620,10 @@
             once(proj_sum.shape),
             once(qkv_keep.shape),
             once(qkv_got.shape),
+            HBM,
+            HBM,
+            HBM,
+            HBM,
             HBM,
             HBM,
         ],
@@ -1637,6 +1645,10 @@
         ),
         scratch_shapes=[
             vmem((2, width), f32),
+            vmem(mine.shape, bf16),
+            vmem(other.shape, bf16),
+            vmem(weight.shape, bf16),
+            vmem(weight_other.shape, bf16),
             vmem((half, width), bf16),
             vmem((half, width), f32),
             vmem((half, width), bf16),
@@ -1646,7 +1658,7 @@
             vmem((bits, 1, size), f32),
             vmem((2 * tiles + 1, rows, FF_TILE), bf16),
             vmem((2 * tiles + 1, rows, FF_TILE), bf16),
-            dma(2),
+            dma(6),
             dma(2),
             dma(2),
             dma(2),
@@ -1660,11 +1672,7 @@
         ),
         name="input_backward",
     )(
-        mine,
-        other,
         other_end,
-        weight,
-        weight_other,
         gain[None, :],
         vectors,
         down_sum,
@@ -1672,6 +1680,10 @@
         proj_sum,
         qkv_keep,
         qkv_got,
+        mine,
+        other,
+        weight,
+        weight_other,
         patches,
         residual_grad,
     )

time: 327 us -> 321 us (0.982)
  Pallas kernels: 315 us -> 310 us
where the time goes in v2:
time: 321 us; the launch traced here: 319 us
  Pallas kernels  310 us (97%)
  other arithmetic  4 us (1%)
    pallas_call x1, Pallas kernels, feed_forward(): pl.pallas_call(feed_kernel, grid=(4 * tiles + 2,), in_specs=[once((column...  112 us
    pallas_call x1, Pallas kernels, attend_backward(): pl.pallas_call(attend_back_kernel, grid=(heads,), out_shape=(jax.ShapeDty...  74.1 us
    pallas_call x1, Pallas kernels, attend_forward(): pl.pallas_call(attend_kernel, grid=(3 + heads,), out_shape=(jax.ShapeDtyp...  60.3 us
    pallas_call x1, Pallas kernels, input_backward(): pl.pallas_call(functools.partial(input_back_kernel, bits), grid=(2,), in_...  57 us

profile of v2, /device:TPU:0, one launch (start us, length us, event | category | flops | bytes accessed | tf_op | source)
XLA Modules:
  0.0 319.0 jit_solution(11216224957449157616)
XLA Ops:
  1.9 0.1 fusion.6
  2.1 0.1 fusion.8
  2.3 1.6 fusion
  4.6 0.7 select_convert_fusion.qm_ref
  5.3 0.6 fusion.2.km_ref
  5.9 60.3 %attend_forward.1 = (bf16[1040,1568]{1,0:T(8,128)(2,1)}, bf16[3,512,1568]{2,1,0:T(8,128)(2,1)}, bf16[512,1568]{1,0:T(8,128)(2,1)}, bf16[512,784]{1,0:T(8,128)(2,...) custom-call(bf16[1568,1024]{1,0:T(8,128)(2,1)} %x_hbm.1, ...), custom_call_target="tpu_custom_call" | custom-call | flops 25073549312 | bytes 60000000 | tf_op jit(solution)/shard_map/attend_forward/pallas_call | solution.py:415
  66.2 112.4 %feed_forward.1 = (f32[784,1024]{1,0:T(8,128)}, bf16[512,784]{1,0:T(8,128)(2,1)}, bf16[512,784]{1,0:T(8,128)(2,1)}, f32[4,1024]{1,0:T(4,128)}, f32[8,1,512]{2,1,...) custom-call(bf16[512,784]{1,0:T(8,128)(2,1)} %get-tuple-element.70.a, ...), custom_call_target="tpu_custom_call", output_to_operand_aliasing={{11}: (14, {})} | custom-call | flops 39460012032 | bytes 60000000 | tf_op jit(solution)/shard_map/feed_forward/pallas_call | solution.py:1225
  178.6 0.0 copy-start.1
  178.6 0.0 copy-start
  178.6 74.1 %attend_backward.1 = (bf16[3,512,784]{2,1,0:T(8,128)(2,1)}, bf16[3,8,64,512]{3,2,1,0:T(8,128)(2,1)}, f32[3,512]{1,0:T(4,128)}, f32[8,1,64,512]{3,2,1,0:T(8,128)}...) custom-call(bf16[8,1568,1568]{2,1,0:T(8,128)(2,1)} %get-tuple-elemen, ...), custom_call_target="tpu_custom_call", output_to_operand_aliasing={{9}: (15, {})} | custom-call | flops 40282095616 | bytes 39337984 | tf_op jit(solution)/shard_map/attend_backward/pallas_call | solution.py:774
  252.7 0.7 copy.32
  253.4 0.0 copy-done.1
  253.5 0.0 copy-done
  253.6 0.7 maximum_maximum_fusion.vector_ref
  254.3 57.0 %input_backward.1 = (f32[1,9728]{1,0:T(1,128)}, f32[64,2048]{1,0:T(8,128)}, f32[64,2048]{1,0:T(8,128)}, f32[64,512]{1,0:T(8,128)}, f32[3,64,512]{2,1,0:T(8,128)}, /*index=5*/bf16[1568,1024]{1,0:T(8,128)(2,1)}) custom-call(bf16[16,2048]{1,0:T(8,128)(2,1)} %get-tuple-element.84.other_end_ref, f32[1,1024]{1,0:T(1,128)} %bitcast.34, ...), custom_call_target="tpu_custom_call" | custom-call | flops 4932501504 | bytes 20000000 | tf_op jit(solution)/shard_map/input_backward/pallas_call | solution.py:1611
  311.3 5.9 %results.1 = (f32[64,2048]{1,0:T(8,128)}, f32[64,2048]{1,0:T(8,128)}, f32[64,512]{1,0:T(8,128)}, f32[3,64,512]{2,1,0:T(8,128)}, bf16[1568,1024]{1,0:T(8,128)(2,1...) custom-call(f32[1,9728]{1,0:T(1,128)} %get-tuple-element.97.vector_r, ...), custom_call_target="tpu_custom_call" | custom-call | tf_op jit(solution)/shard_map/results/pallas_call | solution.py:1715
  317.3 1.3 reshape_reshape.3
  (9 shorter events, 0.1 us)
Async XLA Ops:
  178.6 74.8 %copy-start.1 = (f32[8,1,512]{2,1,0:T(1,128)S(1)}, f32[8,1,512]{2,1,0:T(1,128)}, u32[]{:S(2)}) copy-start(f32[8,1,512]{2,1,0:T(1,128)} %get-tuple-element.86) | copy-start | bytes 49156
  178.6 74.9 %copy-start = (f32[4,1024]{1,0:T(4,128)S(1)}, f32[4,1024]{1,0:T(4,128)}, u32[]{:S(2)}) copy-start(f32[4,1024]{1,0:T(4,128)} %get-tuple-element.85) | copy-start | bytes 49156

commit v3 on v2

--- a/solution.py
+++ b/solution.py
@@ -1700,30 +1700,28 @@
         for source, target in zip(sources[:-2], targets[:-2]):
             target[...] = source[...]
         begin = 0
-        for size, target in zip(sizes, refs[2 * count :]):
-            for row in range(size // 128):
-                at = pl.ds(begin + row * 128, 128)
-                target[row : row + 1, :] = vector_ref[:, at]
-            begin += size
+        for (rows, columns), target in zip(sizes, refs[2 * count :]):
+            for row in range(rows):
+                target[row : row + 1, :] = vector_ref[:, pl.ds(begin, columns)]
+                begin += columns
 
 
 def results(vectors, sizes, arrays, rows):
     step = rows[0].shape[0] // RESULT_STEPS
     long_block = pl.BlockSpec((step, rows[0].shape[1]), lambda i: (i, 0))
     specs = [once(x.shape) for x in arrays] + [long_block] * len(rows)
-    shapes = [(size // 128, 128) for size in sizes]
     out = pl.pallas_call(
         functools.partial(result_kernel, sizes),
         grid=(RESULT_STEPS,),
         in_specs=[once(vectors.shape)] + specs,
-        out_specs=specs + [once(x) for x in shapes],
+        out_specs=specs + [once(x) for x in sizes],
         out_shape=[jax.ShapeDtypeStruct(x.shape, x.dtype) for x in list(arrays) + list(rows)]
-        + [jax.ShapeDtypeStruct(x, f32) for x in shapes],
+        + [jax.ShapeDtypeStruct(x, f32) for x in sizes],
         compiler_params=params(),
         name="results",
     )(vectors, *arrays, *rows)
     count = len(arrays) + len(rows)
-    return out[:count], [x.reshape(-1) for x in out[count:]]
+    return out[:count], list(out[count:])
 
 
 def on_device(
@@ -1871,19 +1869,22 @@
         patches,
         residual_grad,
     )
-    sizes = [width] * 6 + [hidden, 3 * local_width]
+    sizes = [(width // 128, 128)] * 6 + [(hidden // 128, 128), (3, local_width)]
     (down_grad, up_grad, proj_grad, qkv_grad, block_out, patch_grad), pieces = results(
         vectors, sizes, [down_grad, up_grad, proj_grad, qkv_grad], [block_out, patch_grad]
     )
-    attn_gain_grad, attn_shift_grad, mlp_gain_grad, mlp_shift_grad = pieces[:4]
-    proj_bias_grad, down_bias_grad, up_bias_grad, qkv_bias_grad = pieces[4:]
+    qkv_bias_grad = pieces.pop()
+    attn_gain_grad, attn_shift_grad, mlp_gain_grad, mlp_shift_grad = (
+        x.reshape(-1) for x in pieces[:4]
+    )
+    proj_bias_grad, down_bias_grad, up_bias_grad = (x.reshape(-1) for x in pieces[4:])
     return (
         block_out,
         patch_grad,
         attn_gain_grad,
         attn_shift_grad,
         jnp.transpose(qkv_grad, (1, 0, 2)),
-        qkv_bias_grad.reshape(3, local_width),
+        qkv_bias_grad,
         proj_grad.T,
         proj_bias_grad,
         mlp_gain_grad,

time: 321 us -> 320 us (level)
  no operation moved by 1% of the time
where the time goes in v3:
time: 320 us; the launch traced here: 318 us
  Pallas kernels  310 us (97%)
  other arithmetic  4 us (1%)
    pallas_call x1, Pallas kernels, feed_forward(): pl.pallas_call(feed_kernel, grid=(4 * tiles + 2,), in_specs=[once((column...  112 us
    pallas_call x1, Pallas kernels, attend_backward(): pl.pallas_call(attend_back_kernel, grid=(heads,), out_shape=(jax.ShapeDty...  74.1 us
    pallas_call x1, Pallas kernels, attend_forward(): pl.pallas_call(attend_kernel, grid=(3 + heads,), out_shape=(jax.ShapeDtyp...  60.3 us
    pallas_call x1, Pallas kernels, input_backward(): pl.pallas_call(functools.partial(input_back_kernel, bits), grid=(2,), in_...  57 us

profile of v3, /device:TPU:0, one launch (start us, length us, event | category | flops | bytes accessed | tf_op | source)
XLA Modules:
  0.0 317.7 jit_solution(4034238738890155999)
XLA Ops:
  1.9 0.1 fusion.6
  2.1 0.1 fusion.8
  2.3 1.6 fusion
  4.6 0.7 select_convert_fusion.qm_ref
  5.3 0.6 fusion.2.km_ref
  5.9 60.3 %attend_forward.1 = (bf16[1040,1568]{1,0:T(8,128)(2,1)}, bf16[3,512,1568]{2,1,0:T(8,128)(2,1)}, bf16[512,1568]{1,0:T(8,128)(2,1)}, bf16[512,784]{1,0:T(8,128)(2,...) custom-call(bf16[1568,1024]{1,0:T(8,128)(2,1)} %x_hbm.1, ...), custom_call_target="tpu_custom_call" | custom-call | flops 25073549312 | bytes 60000000 | tf_op jit(solution)/shard_map/attend_forward/pallas_call | solution.py:415
  66.2 112.4 %feed_forward.1 = (f32[784,1024]{1,0:T(8,128)}, bf16[512,784]{1,0:T(8,128)(2,1)}, bf16[512,784]{1,0:T(8,128)(2,1)}, f32[4,1024]{1,0:T(4,128)}, f32[8,1,512]{2,1,...) custom-call(bf16[512,784]{1,0:T(8,128)(2,1)} %get-tuple-element.70.a, ...), custom_call_target="tpu_custom_call", output_to_operand_aliasing={{11}: (14, {})} | custom-call | flops 39460012032 | bytes 60000000 | tf_op jit(solution)/shard_map/feed_forward/pallas_call | solution.py:1225
  178.6 0.0 copy-start.1
  178.6 0.0 copy-start
  178.6 74.1 %attend_backward.1 = (bf16[3,512,784]{2,1,0:T(8,128)(2,1)}, bf16[3,8,64,512]{3,2,1,0:T(8,128)(2,1)}, f32[3,512]{1,0:T(4,128)}, f32[8,1,64,512]{3,2,1,0:T(8,128)}...) custom-call(bf16[8,1568,1568]{2,1,0:T(8,128)(2,1)} %get-tuple-elemen, ...), custom_call_target="tpu_custom_call", output_to_operand_aliasing={{9}: (15, {})} | custom-call | flops 40282095616 | bytes 39337984 | tf_op jit(solution)/shard_map/attend_backward/pallas_call | solution.py:774
  252.7 0.7 copy.32
  253.4 0.0 copy-done.1
  253.5 0.0 copy-done
  253.6 0.7 maximum_maximum_fusion.vector_ref
  254.3 57.0 %input_backward.1 = (f32[1,9728]{1,0:T(1,128)}, f32[64,2048]{1,0:T(8,128)}, f32[64,2048]{1,0:T(8,128)}, f32[64,512]{1,0:T(8,128)}, f32[3,64,512]{2,1,0:T(8,128)}, /*index=5*/bf16[1568,1024]{1,0:T(8,128)(2,1)}) custom-call(bf16[16,2048]{1,0:T(8,128)(2,1)} %get-tuple-element.84.other_end_ref, f32[1,1024]{1,0:T(1,128)} %bitcast.34, ...), custom_call_target="tpu_custom_call" | custom-call | flops 4932501504 | bytes 20000000 | tf_op jit(solution)/shard_map/input_backward/pallas_call | solution.py:1611
  311.3 5.9 %results.1 = (f32[64,2048]{1,0:T(8,128)}, f32[64,2048]{1,0:T(8,128)}, f32[64,512]{1,0:T(8,128)}, f32[3,64,512]{2,1,0:T(8,128)}, bf16[1568,1024]{1,0:T(8,128)(2,1...) custom-call(f32[1,9728]{1,0:T(1,128)} %get-tuple-element.97.vector_r, ...), custom_call_target="tpu_custom_call" | custom-call | tf_op jit(solution)/shard_map/results/pallas_call | solution.py:1713
  (9 shorter events, 0.1 us)
Async XLA Ops:
  178.6 74.8 %copy-start.1 = (f32[8,1,512]{2,1,0:T(1,128)S(1)}, f32[8,1,512]{2,1,0:T(1,128)}, u32[]{:S(2)}) copy-start(f32[8,1,512]{2,1,0:T(1,128)} %get-tuple-element.86) | copy-start | bytes 49156
  178.6 74.9 %copy-start = (f32[4,1024]{1,0:T(4,128)S(1)}, f32[4,1024]{1,0:T(4,128)}, u32[]{:S(2)}) copy-start(f32[4,1024]{1,0:T(4,128)} %get-tuple-element.85) | copy-start | bytes 49156
